TPU v7x, 512 devices: a whole 4x4x16 slice. The times are simulated.
512 devices in a mesh: rows: 64 (over z, y), feat: 8 (over x, core).
Axes of the slice: x: 4, y: 4, z: 16, core: 2. Of those that a mesh axis runs over, the one named last changes fastest.
Arguments:
- feature_table: bfloat16 [393216, 2048], P('rows', 'feat'), may hold values from -0.21875 to 0.21875
- transition_pairs: int32 [393216, 2], P('rows'), may hold values from 0 to 6143
- task_ids: int32 [393216], P('rows'), may hold values from 0 to 63, as said below
- rewards: float32 [393216], P('rows'), may hold values from -6 to 6
Outputs:
- solution: float32 [2048, 64], P('feat')
- direction: float32 [2048, 64], P('feat')
- phi_bar: float32 [64], replicated
Inputs may be any that keep to these rules, and one draw needn't show every extreme that they name: Each row indexes the 6144 states of its own block: row r uses table rows (r // 6144) * 6144 + transition_pairs[r]. `task_ids`: within each aligned block of 6144 rows every task occurs at least once.
All inputs are finite; a program needn't handle non-finite values.
Results may differ from a plain program's by a relative error of at most 0.0003.
Values sent between devices are 32-bit elements; how exact they have to be, the bound alone decides.
No kernel may reach another device: no remote copies, remote signals or barrier semaphores. Data moves between devices by JAX's collectives and lax.ppermute only.
A program may use at most 64 MiB of HBM per device.

v0:
```python
import jax
import jax.numpy as jnp
from jax import lax
from jax.sharding import PartitionSpec as P

TASKS = 64
ITERS = 3


DISCOUNT = 0.95
PRECISE = lax.Precision.HIGHEST


def task_sums(onehot, values):
    return jnp.einsum("rk,r->k", onehot, values, precision=PRECISE)


def per_row(onehot, values):
    return jnp.einsum("rk,k->r", onehot, values, precision=PRECISE)


def rotate(state, left_scale, right_vector, right_scale):
    solution, direction, phi_bar, rho_bar = state
    rotation = jnp.sqrt(rho_bar * rho_bar + left_scale * left_scale)
    cosine = rho_bar / rotation
    sine_part = left_scale / rotation
    theta_term = sine_part * right_scale
    rho_bar = -cosine * right_scale
    phi_term = cosine * phi_bar
    phi_bar = sine_part * phi_bar
    solution = solution + (phi_term / rotation)[None, :] * direction
    direction = right_vector - (theta_term / rotation)[None, :] * direction
    return (solution, direction, phi_bar, rho_bar)


def body(feature_table, transition_pairs, task_ids, rewards):
    local_matrix = feature_table[transition_pairs[:, 0]].astype(
        jnp.float32
    ) - DISCOUNT * feature_table[transition_pairs[:, 1]].astype(jnp.float32)
    onehot = (task_ids[:, None] == jnp.arange(TASKS, dtype=jnp.int32)[None, :]).astype(jnp.float32)

    def back_full(left_values):
        return jnp.einsum(
            "rf,rk->fk", local_matrix, onehot * left_values[:, None], precision=PRECISE
        )

    def back_sum(left_values):
        return lax.psum(back_full(left_values), "rows")

    def left_step(raw_left):
        squares = task_sums(onehot, raw_left * raw_left)
        squares = lax.psum(squares, "rows")
        left_scale = jnp.sqrt(squares)
        left_vector = raw_left * per_row(onehot, 1.0 / left_scale)
        return (left_vector, left_scale, back_sum(left_vector))

    def right_step(raw_right):
        squares = jnp.sum(raw_right * raw_right, axis=0)
        squares = lax.psum(squares, "feat")
        right_scale = jnp.sqrt(squares)
        return (raw_right / right_scale[None, :], right_scale)

    left_vector, left_scale, back = left_step(rewards)
    right_vector, right_scale = right_step(back)
    state = (jnp.zeros_like(right_vector), right_vector, left_scale, right_scale)
    for iteration in range(ITERS):
        product = jnp.dot(local_matrix, right_vector, precision=PRECISE)
        partial_rows = jnp.sum(product * onehot, axis=1)
        raw_left = lax.psum(partial_rows, "feat") - per_row(onehot, right_scale) * left_vector
        left_vector, left_scale, back = left_step(raw_left)
        right_vector, right_scale = right_step(back - left_scale[None, :] * right_vector)
        state = rotate(state, left_scale, right_vector, right_scale)
    solution, direction, phi_bar = (state[0], state[1], state[2])
    return (solution, direction, phi_bar)


def solution(mesh):
    return jax.shard_map(
        body,
        mesh=mesh,
        in_specs=(P("rows", "feat"), P("rows", None), P("rows"), P("rows")),
        out_specs=(P("feat", None), P("feat", None), P()),
        check_vma=False,
    )
```

profile of v0, /device:TPU:1, one launch (start us, length us, event | category | flops | bytes accessed | tf_op | source)
XLA Modules:
  0.0 1825.9 jit_solution(13742893081856878422)
XLA Ops:
  9.1 24.9 %gather_fusion = bf16[6144,256]{1,0:T(8,128)(2,1)} fusion(bf16[6144,256]{1,0:T(8,128)(2,1)S(1)} %copy-done, s32[6144]{0:T(1024)S(1)} %broadcast_clamp_fusion.1), kind=kCustom, calls=%fused_computation | custom fusion | bytes 6316032 | tf_op jit(solution)/shard_map/gather | solution.py:37
  34.0 24.9 %gather_fusion.1 = bf16[6144,256]{1,0:T(8,128)(2,1)} fusion(bf16[6144,256]{1,0:T(8,128)(2,1)S(1)} %copy-done, s32[6144]{0:T(1024)S(1)} %broadcast_clamp_fusion), kind=kCustom, calls=%fused_computation.1 | custom fusion | bytes 6316032 | tf_op jit(solution)/shard_map/gather | solution.py:39
  59.7 122.9 %psum.105 = f32[64]{0:T(128)S(1)} all-reduce(f32[64]{0:T(128)S(1)} %fusion.22), channel_id=1, replica_groups=mesh['rows'=64,'feat'=8] {'rows'}, use_global_device_ids=true, to_apply=%region_0.0 | all-reduce | flops 64 | bytes 512 | tf_op jit(solution)/shard_map/psum | solution.py:52
  183.2 7.2 fusion.3
  190.5 267.8 %all-reduce.5.cloned.1.call-done = f32[256,64]{0,1:T(8,128)} async-done(((f32[256,64]{0,1:T(8,128)}), f32[256,64]{0,1:T(8,128)}) %all-reduce.5.cloned.1.call-update) | async-done | bytes 65552 | tf_op jit(solution)/shard_map/psum | solution.py:48
  459.2 22.7 %psum.107 = f32[64]{0:T(128)S(1)} all-reduce(f32[64]{0:T(128)S(1)} %multiply_reduce_fusion.3), channel_id=1, replica_groups=mesh['rows'=64,'feat'=8] {'feat'}, use_global_device_ids=true, to_apply=%region_3.0 | all-reduce | flops 64 | bytes 512 | tf_op jit(solution)/shard_map/psum | solution.py:59
  482.5 9.8 fusion.19
  492.3 20.7 %psum.108 = f32[6144]{0:T(1024)S(1)} all-reduce(f32[6144]{0:T(1024)S(1)} %fusion.19), channel_id=1, replica_groups=mesh['rows'=64,'feat'=8] {'feat'}, use_global_device_ids=true, to_apply=%region_5.0 | all-reduce | flops 6144 | bytes 49152 | tf_op jit(solution)/shard_map/psum | solution.py:69
  513.9 113.3 %psum.109 = f32[64]{0:T(128)S(1)} all-reduce(f32[64]{0:T(128)S(1)} %fusion.23), channel_id=1, replica_groups=mesh['rows'=64,'feat'=8] {'rows'}, use_global_device_ids=true, to_apply=%region_6.0 | all-reduce | flops 64 | bytes 512 | tf_op jit(solution)/shard_map/psum | solution.py:52
  627.8 7.2 fusion.2
  635.1 268.0 %all-reduce.7.cloned.1.call-done = f32[256,64]{0,1:T(8,128)} async-done(((f32[256,64]{0,1:T(8,128)}), f32[256,64]{0,1:T(8,128)}) %all-reduce.7.cloned.1.call-update) | async-done | bytes 65552 | tf_op jit(solution)/shard_map/psum | solution.py:48
  904.1 22.7 %psum.111 = f32[64]{0:T(128)S(1)} all-reduce(f32[64]{0:T(128)S(1)} %multiply_reduce_fusion.2), channel_id=1, replica_groups=mesh['rows'=64,'feat'=8] {'feat'}, use_global_device_ids=true, to_apply=%region_9.0 | all-reduce | flops 64 | bytes 512 | tf_op jit(solution)/shard_map/psum | solution.py:59
  928.4 9.8 fusion.20
  938.2 20.7 %psum.112 = f32[6144]{0:T(1024)S(1)} all-reduce(f32[6144]{0:T(1024)S(1)} %fusion.20), channel_id=1, replica_groups=mesh['rows'=64,'feat'=8] {'feat'}, use_global_device_ids=true, to_apply=%region_11.0 | all-reduce | flops 6144 | bytes 49152 | tf_op jit(solution)/shard_map/psum | solution.py:69
  959.7 113.3 %psum.113 = f32[64]{0:T(128)S(1)} all-reduce(f32[64]{0:T(128)S(1)} %fusion.24), channel_id=1, replica_groups=mesh['rows'=64,'feat'=8] {'rows'}, use_global_device_ids=true, to_apply=%region_12.0 | all-reduce | flops 64 | bytes 512 | tf_op jit(solution)/shard_map/psum | solution.py:52
  1073.6 7.2 fusion.1
  1080.9 268.0 %all-reduce.9.cloned.1.call-done = f32[256,64]{0,1:T(8,128)} async-done(((f32[256,64]{0,1:T(8,128)}), f32[256,64]{0,1:T(8,128)}) %all-reduce.9.cloned.1.call-update) | async-done | bytes 65552 | tf_op jit(solution)/shard_map/psum | solution.py:48
  1349.9 22.7 %psum.115 = f32[64]{0:T(128)S(1)} all-reduce(f32[64]{0:T(128)S(1)} %multiply_reduce_fusion.1), channel_id=1, replica_groups=mesh['rows'=64,'feat'=8] {'feat'}, use_global_device_ids=true, to_apply=%region_15.0 | all-reduce | flops 64 | bytes 512 | tf_op jit(solution)/shard_map/psum | solution.py:59
  1373.2 9.8 fusion.21
  1383.1 20.7 %psum.116 = f32[6144]{0:T(1024)S(1)} all-reduce(f32[6144]{0:T(1024)S(1)} %fusion.21), channel_id=1, replica_groups=mesh['rows'=64,'feat'=8] {'feat'}, use_global_device_ids=true, to_apply=%region_17.0 | all-reduce | flops 6144 | bytes 49152 | tf_op jit(solution)/shard_map/psum | solution.py:69
  1404.6 113.4 %psum.117 = f32[64]{0:T(128)S(1)} all-reduce(f32[64]{0:T(128)S(1)} %fusion.25), channel_id=1, replica_groups=mesh['rows'=64,'feat'=8] {'rows'}, use_global_device_ids=true, to_apply=%region_18.0 | all-reduce | flops 64 | bytes 512 | tf_op jit(solution)/shard_map/psum | solution.py:52
  1518.6 7.2 fusion
  1526.4 267.5 %all-reduce.11.cloned.1.call-done = f32[256,64]{0,1:T(8,128)} async-done(((f32[256,64]{0,1:T(8,128)}), f32[256,64]{0,1:T(8,128)}) %all-reduce.11.cloned.1.call-update) | async-done | bytes 65552 | tf_op jit(solution)/shard_map/psum | solution.py:48
  1794.9 22.7 %psum.119 = f32[64]{0:T(128)S(1)} all-reduce(f32[64]{0:T(128)S(1)} %multiply_reduce_fusion), channel_id=1, replica_groups=mesh['rows'=64,'feat'=8] {'feat'}, use_global_device_ids=true, to_apply=%region_21.0 | all-reduce | flops 64 | bytes 512 | tf_op jit(solution)/shard_map/psum | solution.py:59
  (53 shorter events, 16.7 us)
Async XLA Ops:
  7.2 1.9 copy-start
  7.2 451.1 %all-reduce.5.cloned.1.call-start = ((), (), s32[]{:S(2)}) async-start(), calls=%async_computation | async-start | bytes 131072 | tf_op jit(solution)/shard_map/psum | solution.py:48
  34.0 24.9 %copy-start.3 = (f32[6144]{0:T(1024)S(1)}, f32[6144]{0:T(1024)}, u32[]{:S(2)}) copy-start(f32[6144]{0:T(1024)} %param.7) | copy-start | bytes 73732
  34.0 24.9 %copy-start.4 = (s32[6144]{0:T(1024)S(1)}, s32[6144]{0:T(1024)}, u32[]{:S(2)}) copy-start(s32[6144]{0:T(1024)} %param.6) | copy-start | bytes 73732
  190.4 712.6 %all-reduce.7.cloned.1.call-start = ((), (), s32[]{:S(2)}) async-start(), calls=%async_computation.1 | async-start | bytes 131072 | tf_op jit(solution)/shard_map/psum | solution.py:48
  627.8 275.3 %copy-start.1 = (f32[256,64]{0,1:T(8,128)S(1)}, f32[256,64]{0,1:T(8,128)}, u32[]{:S(2)}) copy-start(f32[256,64]{0,1:T(8,128)} %all-reduce.5.cloned.1.call-done) | copy-start | bytes 196612
  635.0 713.9 %all-reduce.9.cloned.1.call-start = ((), (), s32[]{:S(2)}) async-start(), calls=%async_computation.2 | async-start | bytes 131072 | tf_op jit(solution)/shard_map/psum | solution.py:48
  1080.9 713.0 %all-reduce.11.cloned.1.call-start = ((), (), s32[]{:S(2)}) async-start(), calls=%async_computation.3 | async-start | bytes 131072 | tf_op jit(solution)/shard_map/psum | solution.py:48
  1518.6 275.3 %copy-start.2 = (f32[256,64]{0,1:T(8,128)S(1)}, f32[256,64]{0,1:T(8,128)}, u32[]{:S(2)}) copy-start(f32[256,64]{0,1:T(8,128)} %all-reduce.9.cloned.1.call-done) | copy-start | bytes 196612
Sparse Core Ops, SparseCore 0:
  190.6 267.6 all-reduce.4
  635.2 267.8 all-reduce.6
  1081.0 267.8 all-reduce.8
  1526.0 267.8 all-reduce.10
where the time goes:
time: 1830 us
  waiting for transfers between devices  1070 us (58%)
  blocking collectives  616 us (34%)
  matrix products  65.6 us (4%)
  local copies, waits for them, and re-layouts  50.7 us (3%)
    psum x4, waiting for transfers between devices, back_sum(): return lax.psum(back_full(left_values), 'rows')  1070 us
    psum x4, blocking collectives, left_step(): squares = lax.psum(squares, 'rows')  463 us
    psum x4, blocking collectives, right_step(): squares = lax.psum(squares, 'feat')  90.9 us
    psum x3, blocking collectives, body(): lax.psum(partial_rows, 'feat') - per_row(onehot, right_scale) * left_vector  62.2 us
  transfers between devices with their start and end apart: 4, of which 4 were waited for; matrix products, arithmetic and copies ran while one was open for 0% of the time, Pallas kernels for 0%

commit v1 on v0

v1 whole, which is shorter than its diff:
```python
import functools

import jax
import jax.numpy as jnp
from jax import lax
from jax.experimental import pallas as pl
from jax.experimental.pallas import tpu as pltpu
from jax.sharding import Mesh
from jax.sharding import PartitionSpec as P

TASKS = 64
ITERS = 3
DISCOUNT = 0.95

ROWS = 6144
FEATS = 256
GATHER = 32
CHUNK = 512
LINE = ROWS + 128

F32 = jnp.float32
BF16 = jnp.bfloat16
VMEM = pl.BlockSpec(memory_space=pltpu.VMEM)
SMEM = pl.BlockSpec(memory_space=pltpu.SMEM)


def shaped(*shape, dtype=F32):
    return jax.ShapeDtypeStruct(shape, dtype)


def call(kernel, operands, outs, scratch=(), specs=None, limit=24):
    return pl.pallas_call(
        kernel,
        out_shape=tuple(outs),
        in_specs=specs or [VMEM] * len(operands),
        out_specs=tuple([VMEM] * len(outs)),
        scratch_shapes=list(scratch),
        compiler_params=pltpu.CompilerParams(vmem_limit_bytes=limit * 2**20),
    )(*operands)


def split3(values):
    high = values.astype(BF16)
    rest = values - high.astype(F32)
    middle = rest.astype(BF16)
    low = (rest - middle.astype(F32)).astype(BF16)
    return high, middle, low


def diagonal():
    shape = (TASKS, 128)
    return lax.broadcasted_iota(jnp.int32, shape, 0) == lax.broadcasted_iota(jnp.int32, shape, 1)


def to_row(column):
    return jnp.sum(jnp.where(diagonal(), column, 0.0), axis=0, keepdims=True)


def to_column(row):
    return jnp.sum(jnp.where(diagonal(), row, 0.0), axis=1, keepdims=True)


def task_mask(task_ref, start):
    tasks = task_ref[:, pl.ds(start, CHUNK)]
    return lax.broadcasted_iota(jnp.int32, (TASKS, CHUNK), 0) == tasks


def add_back(chunk_index, mask, raw, ab_ref, acc_ref, squares):
    start = chunk_index * CHUNK
    parts = [jnp.where(mask, part.astype(F32), 0.0).astype(BF16) for part in split3(raw)]
    term = jnp.dot(
        jnp.concatenate(parts, axis=0),
        ab_ref[pl.ds(start, CHUNK), :],
        preferred_element_type=F32,
    )
    if chunk_index == 0:
        acc_ref[...] = term
    else:
        acc_ref[...] += term
    squared = jnp.where(mask, raw * raw, 0.0)
    for tile in range(CHUNK // 128):
        squares = squares + squared[:, tile * 128 : (tile + 1) * 128]
    return squares


def write_pieces(acc_ref, squares, piece_ref):
    total = acc_ref[0:64, :] + acc_ref[64:128, :] + acc_ref[128:192, :]
    back = total[:, :FEATS] - DISCOUNT * total[:, FEATS:]
    line = jnp.broadcast_to(to_row(jnp.sum(squares, axis=1, keepdims=True)), (8, 128))
    for piece in range(4):
        piece_ref[piece, 0:16, :] = back[16 * piece : 16 * piece + 16, :128]
        piece_ref[piece, 16:32, :] = back[16 * piece : 16 * piece + 16, 128:]
        piece_ref[piece, 32:40, :] = line


def start_kernel(first_ref, second_ref, table_ref, task_ref, rewards_ref, ab_ref, piece_ref, wide, left, right, acc):
    def widen(step, carry):
        base = pl.multiple_of(step * 16, 16)
        rows = table_ref[pl.ds(base, 16), :].astype(F32)
        wide[pl.ds(2 * base, 16, 2), :] = rows[:, :128]
        wide[pl.ds(2 * base + 1, 16, 2), :] = rows[:, 128:]
        return carry

    lax.fori_loop(0, ROWS // 16, widen, 0, unroll=4)

    def gather(step, carry):
        base = pl.multiple_of(step * GATHER, GATHER)
        for row in range(GATHER):
            current = pl.multiple_of(2 * first_ref[base + row], 2)
            following = pl.multiple_of(2 * second_ref[base + row], 2)
            left[2 * row : 2 * row + 2, :] = wide[pl.ds(current, 2), :]
            right[2 * row : 2 * row + 2, :] = wide[pl.ds(following, 2), :]
        for half in range(2):
            lanes = 128 * half
            ab_ref[pl.ds(base, GATHER), lanes : lanes + 128] = left[pl.ds(half, GATHER, 2), :].astype(BF16)
            ab_ref[pl.ds(base, GATHER), FEATS + lanes : FEATS + lanes + 128] = right[
                pl.ds(half, GATHER, 2), :
            ].astype(BF16)
        return carry

    lax.fori_loop(0, ROWS // GATHER, gather, 0)

    squares = jnp.zeros((TASKS, 128), F32)
    for index in range(ROWS // CHUNK):
        start = index * CHUNK
        raw = rewards_ref[:, pl.ds(start, CHUNK)]
        squares = add_back(index, task_mask(task_ref, start), raw, ab_ref, acc, squares)
    write_pieces(acc, squares, piece_ref)


def sum_kernel(copies, in_ref, out_ref):
    total = in_ref[0]
    for index in range(1, in_ref.shape[0]):
        total = total + in_ref[index]
    for index in range(copies):
        out_ref[index] = total


def raw_right_of(pieces_ref, right_ref):
    low = jnp.concatenate([pieces_ref[piece, 0:16, :] for piece in range(4)], axis=0)
    high = jnp.concatenate([pieces_ref[piece, 16:32, :] for piece in range(4)], axis=0)
    back = jnp.concatenate([low, high], axis=1)
    left_scale = jnp.sqrt(to_column(pieces_ref[0, 32:33, :]))
    raw_right = back / left_scale
    if right_ref is not None:
        raw_right = raw_right - left_scale * right_ref[...]
    return raw_right, left_scale


def forward_kernel(first, last, *refs):
    refs = list(refs)
    pieces_ref = refs.pop(0)
    right_ref = None if first else refs.pop(0)
    if last:
        line_ref, raw_ref, scale_ref = refs
    else:
        ab_ref, task_ref, line_ref, raw_ref, scale_ref = refs
    raw_right, left_scale = raw_right_of(pieces_ref, right_ref)
    raw_ref[...] = raw_right
    scale_ref[...] = jnp.broadcast_to(left_scale, (TASKS, 128))
    squares = to_row(jnp.sum(raw_right * raw_right, axis=1, keepdims=True))
    copies = line_ref.shape[0]
    if not last:
        weights = jnp.concatenate(
            [jnp.concatenate(split3(raw_right), axis=0), jnp.concatenate(split3(-DISCOUNT * raw_right), axis=0)],
            axis=1,
        )
        for index in range(ROWS // CHUNK):
            start = index * CHUNK
            product = lax.dot_general(
                weights,
                ab_ref[pl.ds(start, CHUNK), :],
                (((1,), (1,)), ((), ())),
                preferred_element_type=F32,
            )
            product = product[0:64] + product[64:128] + product[128:192]
            chosen = jnp.sum(jnp.where(task_mask(task_ref, start), product, 0.0), axis=0, keepdims=True)
            for copy in range(copies):
                line_ref[copy, :, pl.ds(start, CHUNK)] = chosen
    for copy in range(copies):
        line_ref[copy, :, pl.ds(line_ref.shape[2] - 128, 128)] = squares


def rotate(state, left_scale, right_vector, right_scale):
    solution, direction, phi_bar, rho_bar = state
    rotation = jnp.sqrt(rho_bar * rho_bar + left_scale * left_scale)
    cosine = rho_bar / rotation
    sine_part = left_scale / rotation
    theta_term = sine_part * right_scale
    rho_bar = -cosine * right_scale
    phi_term = cosine * phi_bar
    phi_bar = sine_part * phi_bar
    solution = solution + (phi_term / rotation) * direction
    direction = right_vector - (theta_term / rotation) * direction
    return (solution, direction, phi_bar, rho_bar)


def right_scale_of(line_ref):
    total = line_ref[0, :, pl.ds(line_ref.shape[2] - 128, 128)]
    for index in range(1, line_ref.shape[0]):
        total = total + line_ref[index, :, pl.ds(line_ref.shape[2] - 128, 128)]
    return jnp.sqrt(to_column(total))


def read_state(refs):
    solution, direction, phi_bar, rho_bar = refs
    return (solution[...], direction[...], phi_bar[:, 0:1], rho_bar[:, 0:1])


def back_kernel(first, *refs):
    refs = list(refs)
    line_ref, task_ref, left_ref, ab_ref, raw_ref, scale_ref = refs[:6]
    refs = refs[6:]
    old_state = None if first else read_state(refs[:4])
    refs = refs if first else refs[4:]
    piece_ref, new_left_ref, right_ref, solution_ref, direction_ref, phi_ref, rho_ref, acc = refs
    left_scale = scale_ref[:, 0:1]
    right_scale = right_scale_of(line_ref)
    right_vector = raw_ref[...] / right_scale
    by_product = 1.0 / right_scale
    by_left = right_scale / left_scale

    squares = jnp.zeros((TASKS, 128), F32)
    for index in range(ROWS // CHUNK):
        start = index * CHUNK
        product = line_ref[0, :, pl.ds(start, CHUNK)]
        for other in range(1, line_ref.shape[0]):
            product = product + line_ref[other, :, pl.ds(start, CHUNK)]
        mask = task_mask(task_ref, start)
        raw = product * jnp.sum(jnp.where(mask, by_product, 0.0), axis=0, keepdims=True)
        raw = raw - left_ref[:, pl.ds(start, CHUNK)] * jnp.sum(jnp.where(mask, by_left, 0.0), axis=0, keepdims=True)
        new_left_ref[:, pl.ds(start, CHUNK)] = raw
        squares = add_back(index, mask, raw, ab_ref, acc, squares)
    write_pieces(acc, squares, piece_ref)

    right_ref[...] = right_vector
    if first:
        state = (jnp.zeros_like(right_vector), right_vector, left_scale, right_scale)
    else:
        state = rotate(old_state, left_scale, right_vector, right_scale)
    solution_ref[...] = state[0]
    direction_ref[...] = state[1]
    phi_ref[...] = jnp.broadcast_to(state[2], (TASKS, 128))
    rho_ref[...] = jnp.broadcast_to(state[3], (TASKS, 128))


def end_kernel(line_ref, raw_ref, scale_ref, *refs):
    old_state = read_state(refs[:4])
    solution_ref, direction_ref, phi_ref = refs[4:]
    right_scale = right_scale_of(line_ref)
    state = rotate(old_state, scale_ref[:, 0:1], raw_ref[...] / right_scale, right_scale)
    solution_ref[...] = state[0].T
    direction_ref[...] = state[1].T
    phi_ref[...] = to_row(state[2])[:, :TASKS]


def exchange(array, axes):
    return lax.all_to_all(array, axes, 0, 0)


def summed(array, copies):
    return call(functools.partial(sum_kernel, copies), [array], [shaped(copies, 40, 128)], limit=8)[0]


def rows_sum(pieces, sizes):
    pieces = summed(exchange(pieces, "y"), sizes["z"])
    pieces = summed(exchange(pieces, "z"), sizes["y"])
    return exchange(pieces, "y")


def body(sizes, feature_table, transition_pairs, task_ids, rewards):
    tasks = task_ids.reshape(1, ROWS)
    left = rewards.reshape(1, ROWS)
    peers = sizes["x"] * sizes["core"]
    feat = ("x", "core")
    vectors = [shaped(TASKS, FEATS), shaped(TASKS, 128)]

    ab, pieces = call(
        start_kernel,
        [transition_pairs[:, 0], transition_pairs[:, 1], feature_table, tasks, left],
        [shaped(ROWS, 2 * FEATS, dtype=BF16), shaped(4, 40, 128)],
        scratch=[
            pltpu.VMEM((2 * ROWS, 128), F32),
            pltpu.VMEM((2 * GATHER, 128), F32),
            pltpu.VMEM((2 * GATHER, 128), F32),
            pltpu.VMEM((3 * TASKS, 2 * FEATS), F32),
        ],
        specs=[SMEM, SMEM, VMEM, VMEM, VMEM],
        limit=32,
    )
    pieces = rows_sum(pieces, sizes)
    line, raw, scale = call(
        functools.partial(forward_kernel, True, False),
        [pieces, ab, tasks],
        [shaped(peers, 1, LINE)] + vectors,
    )
    state = []
    for iteration in range(ITERS):
        line = exchange(line, feat)
        pieces, left, right, *state = call(
            functools.partial(back_kernel, iteration == 0),
            [line, tasks, left, ab, raw, scale] + state,
            [shaped(4, 40, 128), shaped(1, ROWS), shaped(TASKS, FEATS)]
            + [shaped(TASKS, FEATS)] * 2
            + [shaped(TASKS, 128)] * 2,
            scratch=[pltpu.VMEM((3 * TASKS, 2 * FEATS), F32)],
        )
        pieces = rows_sum(pieces, sizes)
        last = iteration == ITERS - 1
        line, raw, scale = call(
            functools.partial(forward_kernel, False, last),
            [pieces, right] + ([] if last else [ab, tasks]),
            [shaped(peers, 1, 128 if last else LINE)] + vectors,
        )
    line = exchange(line, feat)
    solution, direction, phi_bar = call(
        end_kernel,
        [line, raw, scale] + state,
        [shaped(FEATS, TASKS), shaped(FEATS, TASKS), shaped(1, TASKS)],
    )
    return (solution, direction, phi_bar.reshape(TASKS))


def solution(mesh):
    names = ("z", "y", "x", "core")
    grid = Mesh(mesh.devices.reshape(16, 4, 4, 2), names)
    sizes = dict(zip(names, grid.devices.shape))
    rows, feat = ("z", "y"), ("x", "core")
    return jax.shard_map(
        functools.partial(body, sizes),
        mesh=grid,
        in_specs=(P(rows, feat), P(rows, None), P(rows), P(rows)),
        out_specs=(P(feat, None), P(feat, None), P()),
        check_vma=False,
    )
```

time: 1830 us -> 254 us (0.14)
  waiting for transfers between devices: 1070 us -> 0 us
  blocking collectives: 616 us -> 215 us
  matrix products: 65.6 us -> 0 us
  local copies, waits for them, and re-layouts: 50.7 us -> 5.7 us
  Pallas kernels: 0 us -> 32 us
    psum x4 -> x0, waiting for transfers between devices: 1070 us -> none  [back_sum(): return lax.psum(back_full(left_values), 'rows')]
    psum x11 -> x0, blocking collectives: 616 us -> none  [the longest x4 463 us: left_step(): squares = lax.psum(squares, 'rows')]
    all_to_all x0 -> x16, blocking collectives: none -> 215 us  [exchange(): return lax.all_to_all(array, axes, 0, 0)]
    dot_general x18 -> x0, matrix products: 65.6 us -> none  [the longest x3 29.4 us: body(): product = jnp.dot(local_matrix, right_vector, precision=PRECISE)]
    gather x2 -> x0, local copies, waits for them, and re-layouts: 49.8 us -> none  [the longest x1 24.9 us: body(): feature_table[transition_pairs[:, 1]].astype(jnp.float32)]
    pallas_call x0 -> x17, Pallas kernels: none -> 32 us  [call(): pl.pallas_call(kernel, out_shape=tuple(outs), in_specs=specs or [VMEM] *...]
  transfers between devices with their start and end apart: 4 -> 0, of which waited for: 4 -> 0; matrix products, arithmetic and copies ran while one was open for 0% -> 0% of each run, Pallas kernels for 0% -> 0%
where the time goes in v1:
time: 254 us; the launch traced here: 253 us
  blocking collectives  215 us (85%)
  Pallas kernels  32 us (13%)
  local copies, waits for them, and re-layouts  5.7 us (2%)
    all_to_all x16, blocking collectives, exchange(): return lax.all_to_all(array, axes, 0, 0)  215 us
    pallas_call x17, Pallas kernels, call(): pl.pallas_call(kernel, out_shape=tuple(outs), in_specs=specs or [VMEM] *...  32 us

profile of v1, /device:TPU:1, one launch (start us, length us, event | category | flops | bytes accessed | tf_op | source)
XLA Modules:
  0.0 253.4 jit_solution(17970945532318628464)
XLA Ops:
  1.6 1.9 copy-done
  4.9 17.2 %shard_map.67 = (bf16[6144,512]{1,0:T(8,128)(2,1)S(1)}, f32[4,40,128]{2,1,0:T(8,128)S(1)}) custom-call(s32[6144]{0:T(1024)S(1)} %bitcast.15, s32[6144]{0:T(1024)S(1)} %bitcast.14, bf16[6144,256]{1,0:T(8,128)(2,1)S(1)} %copy-done, s32[1,6144]{1,0:T(1,128)S(1)} %bitcast.5, f32[1,6144]{1,0:T(1,128)S(1)} %bitcast.12), custom_call_target="tpu_custom_call" | custom-call | tf_op jit(solution)/shard_map/pallas_call | solution.py:32
  22.1 9.4 %all_to_all.80.in_ref = f32[4,40,128]{2,1,0:T(8,128)S(1)} all-to-all(f32[4,40,128]{2,1,0:T(8,128)S(1)} %get-tuple-element.40), channel_id=1, replica_groups=mesh['z'=16,'y'=4,'x'=4,'core'=2] {'y'}, dimensions={0} | all-to-all | bytes 163840 | tf_op jit(solution)/shard_map/all_to_all | solution.py:258
  31.5 28.4 %all_to_all.81.in_ref = f32[16,40,128]{2,1,0:T(8,128)S(1)} all-to-all(f32[16,40,128]{2,1,0:T(8,128)S(1)} %shard_map.68), channel_id=1, replica_groups=mesh['z'=16,'y'=4,'x'=4,'core'=2] {'z'}, dimensions={0} | all-to-all | bytes 655360 | tf_op jit(solution)/shard_map/all_to_all | solution.py:258
  60.0 7.2 %all_to_all.82.refs_0_ = f32[4,40,128]{2,1,0:T(8,128)S(1)} all-to-all(f32[4,40,128]{2,1,0:T(8,128)S(1)} %shard_map.69), channel_id=1, replica_groups=mesh['z'=16,'y'=4,'x'=4,'core'=2] {'y'}, dimensions={0} | all-to-all | bytes 163840 | tf_op jit(solution)/shard_map/all_to_all | solution.py:258
  67.2 2.3 shard_map.70
  69.5 19.1 %all_to_all.83.refs_0_ = f32[8,1,6272]{2,1,0:T(1,128)S(1)} all-to-all(f32[8,1,6272]{2,1,0:T(1,128)S(1)} %get-tuple-element.42), channel_id=1, replica_groups=mesh['z'=16,'y'=4,'x'=4,'core'=2] {'x','core'}, dimensions={0} | all-to-all | bytes 401408 | tf_op jit(solution)/shard_map/all_to_all | solution.py:258
  88.6 2.1 shard_map.71
  90.7 6.9 %all_to_all.84.in_ref = f32[4,40,128]{2,1,0:T(8,128)S(1)} all-to-all(f32[4,40,128]{2,1,0:T(8,128)S(1)} %get-tuple-element.45), channel_id=1, replica_groups=mesh['z'=16,'y'=4,'x'=4,'core'=2] {'y'}, dimensions={0} | all-to-all | bytes 163840 | tf_op jit(solution)/shard_map/all_to_all | solution.py:258
  97.6 19.2 %all_to_all.85.in_ref = f32[16,40,128]{2,1,0:T(8,128)S(1)} all-to-all(f32[16,40,128]{2,1,0:T(8,128)S(1)} %shard_map.72), channel_id=1, replica_groups=mesh['z'=16,'y'=4,'x'=4,'core'=2] {'z'}, dimensions={0} | all-to-all | bytes 655360 | tf_op jit(solution)/shard_map/all_to_all | solution.py:258
  116.9 7.2 %all_to_all.86.refs_0_ = f32[4,40,128]{2,1,0:T(8,128)S(1)} all-to-all(f32[4,40,128]{2,1,0:T(8,128)S(1)} %shard_map.73), channel_id=1, replica_groups=mesh['z'=16,'y'=4,'x'=4,'core'=2] {'y'}, dimensions={0} | all-to-all | bytes 163840 | tf_op jit(solution)/shard_map/all_to_all | solution.py:258
  124.1 2.2 shard_map.74
  126.3 17.4 %all_to_all.87.refs_0_ = f32[8,1,6272]{2,1,0:T(1,128)S(1)} all-to-all(f32[8,1,6272]{2,1,0:T(1,128)S(1)} %get-tuple-element.47), channel_id=1, replica_groups=mesh['z'=16,'y'=4,'x'=4,'core'=2] {'x','core'}, dimensions={0} | all-to-all | bytes 401408 | tf_op jit(solution)/shard_map/all_to_all | solution.py:258
  143.8 2.2 shard_map.75
  145.9 6.9 %all_to_all.88.in_ref = f32[4,40,128]{2,1,0:T(8,128)S(1)} all-to-all(f32[4,40,128]{2,1,0:T(8,128)S(1)} %get-tuple-element.55), channel_id=1, replica_groups=mesh['z'=16,'y'=4,'x'=4,'core'=2] {'y'}, dimensions={0} | all-to-all | bytes 163840 | tf_op jit(solution)/shard_map/all_to_all | solution.py:258
  152.9 19.2 %all_to_all.89.in_ref = f32[16,40,128]{2,1,0:T(8,128)S(1)} all-to-all(f32[16,40,128]{2,1,0:T(8,128)S(1)} %shard_map.76), channel_id=1, replica_groups=mesh['z'=16,'y'=4,'x'=4,'core'=2] {'z'}, dimensions={0} | all-to-all | bytes 655360 | tf_op jit(solution)/shard_map/all_to_all | solution.py:258
  172.1 7.2 %all_to_all.90.refs_0_ = f32[4,40,128]{2,1,0:T(8,128)S(1)} all-to-all(f32[4,40,128]{2,1,0:T(8,128)S(1)} %shard_map.77), channel_id=1, replica_groups=mesh['z'=16,'y'=4,'x'=4,'core'=2] {'y'}, dimensions={0} | all-to-all | bytes 163840 | tf_op jit(solution)/shard_map/all_to_all | solution.py:258
  179.3 2.2 shard_map.78
  181.6 17.4 %all_to_all.91.refs_0_ = f32[8,1,6272]{2,1,0:T(1,128)S(1)} all-to-all(f32[8,1,6272]{2,1,0:T(1,128)S(1)} %get-tuple-element.57), channel_id=1, replica_groups=mesh['z'=16,'y'=4,'x'=4,'core'=2] {'x','core'}, dimensions={0} | all-to-all | bytes 401408 | tf_op jit(solution)/shard_map/all_to_all | solution.py:258
  199.0 2.6 %shard_map.79 = (f32[4,40,128]{2,1,0:T(8,128)S(1)}, f32[1,6144]{1,0:T(1,128)}, f32[64,256]{1,0:T(8,128)S(1)}, f32[64,256]{1,0:T(8,128)S(1)}, f32[64,256]{1,0:T(8...) custom-call(f32[8,1,6272]{2,1,0:T(1,128)S(1)} %all_to_all.91.refs_0_, s32[1,6144]{1,0:T(1,128)S(1)} %bitcast.11, ...), custom_call_target="tpu_custom_call" | custom-call | tf_op jit(solution)/shard_map/pallas_call | solution.py:32
  201.6 6.9 %all_to_all.92.in_ref = f32[4,40,128]{2,1,0:T(8,128)S(1)} all-to-all(f32[4,40,128]{2,1,0:T(8,128)S(1)} %get-tuple-element.65), channel_id=1, replica_groups=mesh['z'=16,'y'=4,'x'=4,'core'=2] {'y'}, dimensions={0} | all-to-all | bytes 163840 | tf_op jit(solution)/shard_map/all_to_all | solution.py:258
  208.5 19.2 %all_to_all.93.in_ref = f32[16,40,128]{2,1,0:T(8,128)S(1)} all-to-all(f32[16,40,128]{2,1,0:T(8,128)S(1)} %shard_map.80), channel_id=1, replica_groups=mesh['z'=16,'y'=4,'x'=4,'core'=2] {'z'}, dimensions={0} | all-to-all | bytes 655360 | tf_op jit(solution)/shard_map/all_to_all | solution.py:258
  227.7 7.2 %all_to_all.94.refs_0_ = f32[4,40,128]{2,1,0:T(8,128)S(1)} all-to-all(f32[4,40,128]{2,1,0:T(8,128)S(1)} %shard_map.81), channel_id=1, replica_groups=mesh['z'=16,'y'=4,'x'=4,'core'=2] {'y'}, dimensions={0} | all-to-all | bytes 163840 | tf_op jit(solution)/shard_map/all_to_all | solution.py:258
  235.2 16.0 %all_to_all.95.line_ref = f32[8,1,128]{2,1,0:T(1,128)S(1)} all-to-all(f32[8,1,128]{2,1,0:T(1,128)S(1)} %get-tuple-element.67), channel_id=1, replica_groups=mesh['z'=16,'y'=4,'x'=4,'core'=2] {'x','core'}, dimensions={0} | all-to-all | bytes 8192 | tf_op jit(solution)/shard_map/all_to_all | solution.py:258
  (18 shorter events, 5.0 us)
Async XLA Ops:
  1.6 1.9 copy-start
  3.4 0.7 copy-start.1
  4.2 0.7 copy-start.2

commit v2 on v1

--- a/solution.py
+++ b/solution.py
@@ -14,7 +14,9 @@
 
 ROWS = 6144
 FEATS = 256
-GATHER = 32
+GATHER = 128
+PIECES = 8
+SHARE = TASKS // PIECES
 CHUNK = 512
 LINE = ROWS + 128
 
@@ -87,13 +89,14 @@
     total = acc_ref[0:64, :] + acc_ref[64:128, :] + acc_ref[128:192, :]
     back = total[:, :FEATS] - DISCOUNT * total[:, FEATS:]
     line = jnp.broadcast_to(to_row(jnp.sum(squares, axis=1, keepdims=True)), (8, 128))
-    for piece in range(4):
-        piece_ref[piece, 0:16, :] = back[16 * piece : 16 * piece + 16, :128]
-        piece_ref[piece, 16:32, :] = back[16 * piece : 16 * piece + 16, 128:]
-        piece_ref[piece, 32:40, :] = line
-
-
-def start_kernel(first_ref, second_ref, table_ref, task_ref, rewards_ref, ab_ref, piece_ref, wide, left, right, acc):
+    for piece in range(PIECES):
+        rows = slice(SHARE * piece, SHARE * piece + SHARE)
+        piece_ref[piece, 0:SHARE, :] = back[rows, :128]
+        piece_ref[piece, SHARE : 2 * SHARE, :] = back[rows, 128:]
+        piece_ref[piece, 2 * SHARE :, :] = line
+
+
+def gather_kernel(first_ref, second_ref, table_ref, ab_ref, wide, left, right):
     def widen(step, carry):
         base = pl.multiple_of(step * 16, 16)
         rows = table_ref[pl.ds(base, 16), :].astype(F32)
@@ -106,8 +109,8 @@
     def gather(step, carry):
         base = pl.multiple_of(step * GATHER, GATHER)
         for row in range(GATHER):
-            current = pl.multiple_of(2 * first_ref[base + row], 2)
-            following = pl.multiple_of(2 * second_ref[base + row], 2)
+            current = pl.multiple_of(first_ref[base + row], 2)
+            following = pl.multiple_of(second_ref[base + row], 2)
             left[2 * row : 2 * row + 2, :] = wide[pl.ds(current, 2), :]
             right[2 * row : 2 * row + 2, :] = wide[pl.ds(following, 2), :]
         for half in range(2):
@@ -120,6 +123,8 @@
 
     lax.fori_loop(0, ROWS // GATHER, gather, 0)
 
+
+def first_back_kernel(task_ref, rewards_ref, ab_ref, piece_ref, acc):
     squares = jnp.zeros((TASKS, 128), F32)
     for index in range(ROWS // CHUNK):
         start = index * CHUNK
@@ -128,6 +133,27 @@
     write_pieces(acc, squares, piece_ref)
 
 
+def start(pairs, table, tasks, rewards):
+    ab = call(
+        gather_kernel,
+        [2 * pairs[:, 0], 2 * pairs[:, 1], table],
+        [shaped(ROWS, 2 * FEATS, dtype=BF16)],
+        scratch=[
+            pltpu.VMEM((2 * ROWS, 128), F32),
+            pltpu.VMEM((2 * GATHER, 128), F32),
+            pltpu.VMEM((2 * GATHER, 128), F32),
+        ],
+        specs=[SMEM, SMEM, VMEM],
+    )[0]
+    pieces = call(
+        first_back_kernel,
+        [tasks, rewards, ab],
+        [shaped(PIECES, 24, 128)],
+        scratch=[pltpu.VMEM((3 * TASKS, 2 * FEATS), F32)],
+    )[0]
+    return ab, pieces
+
+
 def sum_kernel(copies, in_ref, out_ref):
     total = in_ref[0]
     for index in range(1, in_ref.shape[0]):
@@ -137,10 +163,10 @@
 
 
 def raw_right_of(pieces_ref, right_ref):
-    low = jnp.concatenate([pieces_ref[piece, 0:16, :] for piece in range(4)], axis=0)
-    high = jnp.concatenate([pieces_ref[piece, 16:32, :] for piece in range(4)], axis=0)
+    low = jnp.concatenate([pieces_ref[piece, 0:SHARE, :] for piece in range(PIECES)], axis=0)
+    high = jnp.concatenate([pieces_ref[piece, SHARE : 2 * SHARE, :] for piece in range(PIECES)], axis=0)
     back = jnp.concatenate([low, high], axis=1)
-    left_scale = jnp.sqrt(to_column(pieces_ref[0, 32:33, :]))
+    left_scale = jnp.sqrt(to_column(pieces_ref[0, 2 * SHARE : 2 * SHARE + 1, :]))
     raw_right = back / left_scale
     if right_ref is not None:
         raw_right = raw_right - left_scale * right_ref[...]
@@ -249,8 +275,8 @@
     solution_ref, direction_ref, phi_ref = refs[4:]
     right_scale = right_scale_of(line_ref)
     state = rotate(old_state, scale_ref[:, 0:1], raw_ref[...] / right_scale, right_scale)
-    solution_ref[...] = state[0].T
-    direction_ref[...] = state[1].T
+    solution_ref[...] = state[0]
+    direction_ref[...] = state[1]
     phi_ref[...] = to_row(state[2])[:, :TASKS]
 
 
@@ -259,13 +285,14 @@
 
 
 def summed(array, copies):
-    return call(functools.partial(sum_kernel, copies), [array], [shaped(copies, 40, 128)], limit=8)[0]
+    return call(functools.partial(sum_kernel, copies), [array], [shaped(copies, 24, 128)], limit=8)[0]
 
 
 def rows_sum(pieces, sizes):
-    pieces = summed(exchange(pieces, "y"), sizes["z"])
-    pieces = summed(exchange(pieces, "z"), sizes["y"])
-    return exchange(pieces, "y")
+    near, far = ("zl", "y"), "zh"
+    pieces = summed(exchange(pieces, near), sizes["zh"])
+    pieces = summed(exchange(pieces, far), PIECES)
+    return exchange(pieces, near)
 
 
 def body(sizes, feature_table, transition_pairs, task_ids, rewards):
@@ -275,19 +302,7 @@
     feat = ("x", "core")
     vectors = [shaped(TASKS, FEATS), shaped(TASKS, 128)]
 
-    ab, pieces = call(
-        start_kernel,
-        [transition_pairs[:, 0], transition_pairs[:, 1], feature_table, tasks, left],
-        [shaped(ROWS, 2 * FEATS, dtype=BF16), shaped(4, 40, 128)],
-        scratch=[
-            pltpu.VMEM((2 * ROWS, 128), F32),
-            pltpu.VMEM((2 * GATHER, 128), F32),
-            pltpu.VMEM((2 * GATHER, 128), F32),
-            pltpu.VMEM((3 * TASKS, 2 * FEATS), F32),
-        ],
-        specs=[SMEM, SMEM, VMEM, VMEM, VMEM],
-        limit=32,
-    )
+    ab, pieces = start(transition_pairs, feature_table, tasks, left)
     pieces = rows_sum(pieces, sizes)
     line, raw, scale = call(
         functools.partial(forward_kernel, True, False),
@@ -300,7 +315,7 @@
         pieces, left, right, *state = call(
             functools.partial(back_kernel, iteration == 0),
             [line, tasks, left, ab, raw, scale] + state,
-            [shaped(4, 40, 128), shaped(1, ROWS), shaped(TASKS, FEATS)]
+            [shaped(PIECES, 24, 128), shaped(1, ROWS), shaped(TASKS, FEATS)]
             + [shaped(TASKS, FEATS)] * 2
             + [shaped(TASKS, 128)] * 2,
             scratch=[pltpu.VMEM((3 * TASKS, 2 * FEATS), F32)],
@@ -316,16 +331,16 @@
     solution, direction, phi_bar = call(
         end_kernel,
         [line, raw, scale] + state,
-        [shaped(FEATS, TASKS), shaped(FEATS, TASKS), shaped(1, TASKS)],
+        [shaped(TASKS, FEATS), shaped(TASKS, FEATS), shaped(1, TASKS)],
     )
-    return (solution, direction, phi_bar.reshape(TASKS))
+    return (solution.T, direction.T, phi_bar.reshape(TASKS))
 
 
 def solution(mesh):
-    names = ("z", "y", "x", "core")
-    grid = Mesh(mesh.devices.reshape(16, 4, 4, 2), names)
+    names = ("zh", "zl", "y", "x", "core")
+    grid = Mesh(mesh.devices.reshape(8, 2, 4, 4, 2), names)
     sizes = dict(zip(names, grid.devices.shape))
-    rows, feat = ("z", "y"), ("x", "core")
+    rows, feat = ("zh", "zl", "y"), ("x", "core")
     return jax.shard_map(
         functools.partial(body, sizes),
         mesh=grid,

time: 254 us -> 222 us (0.87)
  blocking collectives: 215 us -> 189 us
  Pallas kernels: 32 us -> 28 us
  local copies, waits for them, and re-layouts: 5.7 us -> 1.89 us
    all_to_all x16, blocking collectives: 215 us -> 189 us  [exchange(): return lax.all_to_all(array, axes, 0, 0)]
    pallas_call x17 -> x18, Pallas kernels: 32 us -> 28 us  [call(): pl.pallas_call(kernel, out_shape=tuple(outs), in_specs=specs or [VMEM] *...]
    unnamed x8 -> x6, local copies, waits for them, and re-layouts: 4.78 us -> 1.89 us
where the time goes in v2:
time: 222 us; the launch traced here: 221 us
  blocking collectives  189 us (85%)
  Pallas kernels  28 us (13%)
    all_to_all x16, blocking collectives, exchange(): return lax.all_to_all(array, axes, 0, 0)  189 us
    pallas_call x18, Pallas kernels, call(): pl.pallas_call(kernel, out_shape=tuple(outs), in_specs=specs or [VMEM] *...  28 us

profile of v2, /device:TPU:1, one launch (start us, length us, event | category | flops | bytes accessed | tf_op | source)
XLA Modules:
  0.0 220.9 jit_solution(5757547195383961982)
XLA Ops:
  1.6 1.9 copy-done
  3.5 11.7 %shard_map.67.ab_ref.refs_1_.refs_3_.refs_2_ = bf16[6144,512]{1,0:T(8,128)(2,1)S(1)} custom-call(s32[6144]{0:T(1024)S(1)} %bitcast.17, s32[6144]{0:T(1024)S(1)} %bitcast.16, bf16[6144,256]{1,0:T(8,128)(2,1)S(1)} %copy-done), custom_call_target="tpu_custom_call" | custom-call | tf_op jit(solution)/shard_map/pallas_call | solution.py:34
  16.6 11.5 %all_to_all.80.in_ref = f32[8,24,128]{2,1,0:T(8,128)S(1)} all-to-all(f32[8,24,128]{2,1,0:T(8,128)S(1)} %shard_map.68), channel_id=1, replica_groups=mesh['zh'=8,'zl'=2,'y'=4,'x'=4,'core'=2] {'zl','y'}, dimensions={0} | all-to-all | bytes 196608 | tf_op jit(solution)/shard_map/all_to_all | solution.py:284
  28.1 26.2 %all_to_all.81.in_ref = f32[8,24,128]{2,1,0:T(8,128)S(1)} all-to-all(f32[8,24,128]{2,1,0:T(8,128)S(1)} %shard_map.69), channel_id=1, replica_groups=mesh['zh'=8,'zl'=2,'y'=4,'x'=4,'core'=2] {'zh'}, dimensions={0} | all-to-all | bytes 196608 | tf_op jit(solution)/shard_map/all_to_all | solution.py:284
  54.4 7.7 %all_to_all.82.refs_0_ = f32[8,24,128]{2,1,0:T(8,128)S(1)} all-to-all(f32[8,24,128]{2,1,0:T(8,128)S(1)} %shard_map.70), channel_id=1, replica_groups=mesh['zh'=8,'zl'=2,'y'=4,'x'=4,'core'=2] {'zl','y'}, dimensions={0} | all-to-all | bytes 196608 | tf_op jit(solution)/shard_map/all_to_all | solution.py:284
  62.1 2.3 %shard_map.71 = (f32[8,1,6272]{2,1,0:T(1,128)S(1)}, f32[64,256]{1,0:T(8,128)S(1)}, f32[64,128]{1,0:T(8,128)S(1)}) custom-call(f32[8,24,128]{2,1,0:T(8,128)S(1)} %all_to_all.82.refs_0_, bf16[6144,512]{1,0:T(8,128)(2,1)S(1)} %shard_map.67.ab_ref.refs_1_.refs_3_.refs_2_, s32[1,6144]{1,0:T(1,128)S(1)} %bitcast.8), custom_call_target="tpu_custom_call" | custom-call | tf_op jit(solution)/shard_map/pallas_call | solution.py:34
  64.3 15.0 %all_to_all.83.refs_0_ = f32[8,1,6272]{2,1,0:T(1,128)S(1)} all-to-all(f32[8,1,6272]{2,1,0:T(1,128)S(1)} %get-tuple-element.38), channel_id=1, replica_groups=mesh['zh'=8,'zl'=2,'y'=4,'x'=4,'core'=2] {'x','core'}, dimensions={0} | all-to-all | bytes 401408 | tf_op jit(solution)/shard_map/all_to_all | solution.py:284
  79.3 2.2 shard_map.72
  81.5 7.7 %all_to_all.84.in_ref = f32[8,24,128]{2,1,0:T(8,128)S(1)} all-to-all(f32[8,24,128]{2,1,0:T(8,128)S(1)} %get-tuple-element.41), channel_id=1, replica_groups=mesh['zh'=8,'zl'=2,'y'=4,'x'=4,'core'=2] {'zl','y'}, dimensions={0} | all-to-all | bytes 196608 | tf_op jit(solution)/shard_map/all_to_all | solution.py:284
  89.2 15.0 %all_to_all.85.in_ref = f32[8,24,128]{2,1,0:T(8,128)S(1)} all-to-all(f32[8,24,128]{2,1,0:T(8,128)S(1)} %shard_map.73), channel_id=1, replica_groups=mesh['zh'=8,'zl'=2,'y'=4,'x'=4,'core'=2] {'zh'}, dimensions={0} | all-to-all | bytes 196608 | tf_op jit(solution)/shard_map/all_to_all | solution.py:284
  104.2 7.7 %all_to_all.86.refs_0_ = f32[8,24,128]{2,1,0:T(8,128)S(1)} all-to-all(f32[8,24,128]{2,1,0:T(8,128)S(1)} %shard_map.74), channel_id=1, replica_groups=mesh['zh'=8,'zl'=2,'y'=4,'x'=4,'core'=2] {'zl','y'}, dimensions={0} | all-to-all | bytes 196608 | tf_op jit(solution)/shard_map/all_to_all | solution.py:284
  111.9 2.2 %shard_map.75 = (f32[8,1,6272]{2,1,0:T(1,128)S(1)}, f32[64,256]{1,0:T(8,128)S(1)}, f32[64,128]{1,0:T(8,128)S(1)}) custom-call(f32[8,24,128]{2,1,0:T(8,128)S(1)} %all_to_all.86.refs_0_, f32[64,256]{1,0:T(8,128)S(1)} %get-tuple-element.42.refs_1_, bf16[6144,512]{1,0:T(8,128)(2,1)S(1)} %shard_map.67.ab_ref.refs_1_.refs_3_.refs_2_, s32[1,6144]{1,0:T(1,128)S(1)} %bitcast.10), custom_call_target="tpu_custom_call" | custom-call | tf_op jit(solution)/shard_map/pallas_call | solution.py:34
  114.1 13.1 %all_to_all.87.refs_0_ = f32[8,1,6272]{2,1,0:T(1,128)S(1)} all-to-all(f32[8,1,6272]{2,1,0:T(1,128)S(1)} %get-tuple-element.43), channel_id=1, replica_groups=mesh['zh'=8,'zl'=2,'y'=4,'x'=4,'core'=2] {'x','core'}, dimensions={0} | all-to-all | bytes 401408 | tf_op jit(solution)/shard_map/all_to_all | solution.py:284
  127.2 2.2 shard_map.76
  129.4 7.7 %all_to_all.88.in_ref = f32[8,24,128]{2,1,0:T(8,128)S(1)} all-to-all(f32[8,24,128]{2,1,0:T(8,128)S(1)} %get-tuple-element.51), channel_id=1, replica_groups=mesh['zh'=8,'zl'=2,'y'=4,'x'=4,'core'=2] {'zl','y'}, dimensions={0} | all-to-all | bytes 196608 | tf_op jit(solution)/shard_map/all_to_all | solution.py:284
  137.1 15.0 %all_to_all.89.in_ref = f32[8,24,128]{2,1,0:T(8,128)S(1)} all-to-all(f32[8,24,128]{2,1,0:T(8,128)S(1)} %shard_map.77), channel_id=1, replica_groups=mesh['zh'=8,'zl'=2,'y'=4,'x'=4,'core'=2] {'zh'}, dimensions={0} | all-to-all | bytes 196608 | tf_op jit(solution)/shard_map/all_to_all | solution.py:284
  152.1 7.7 %all_to_all.90.refs_0_ = f32[8,24,128]{2,1,0:T(8,128)S(1)} all-to-all(f32[8,24,128]{2,1,0:T(8,128)S(1)} %shard_map.78), channel_id=1, replica_groups=mesh['zh'=8,'zl'=2,'y'=4,'x'=4,'core'=2] {'zl','y'}, dimensions={0} | all-to-all | bytes 196608 | tf_op jit(solution)/shard_map/all_to_all | solution.py:284
  159.8 2.2 %shard_map.79 = (f32[8,1,6272]{2,1,0:T(1,128)S(1)}, f32[64,256]{1,0:T(8,128)S(1)}, f32[64,128]{1,0:T(8,128)S(1)}) custom-call(f32[8,24,128]{2,1,0:T(8,128)S(1)} %all_to_all.90.refs_0_, f32[64,256]{1,0:T(8,128)S(1)} %get-tuple-element.52.refs_1_, bf16[6144,512]{1,0:T(8,128)(2,1)S(1)} %shard_map.67.ab_ref.refs_1_.refs_3_.refs_2_, s32[1,6144]{1,0:T(1,128)S(1)} %bitcast.12), custom_call_target="tpu_custom_call" | custom-call | tf_op jit(solution)/shard_map/pallas_call | solution.py:34
  162.0 13.1 %all_to_all.91.refs_0_ = f32[8,1,6272]{2,1,0:T(1,128)S(1)} all-to-all(f32[8,1,6272]{2,1,0:T(1,128)S(1)} %get-tuple-element.53), channel_id=1, replica_groups=mesh['zh'=8,'zl'=2,'y'=4,'x'=4,'core'=2] {'x','core'}, dimensions={0} | all-to-all | bytes 401408 | tf_op jit(solution)/shard_map/all_to_all | solution.py:284
  175.2 2.6 %shard_map.80 = (f32[8,24,128]{2,1,0:T(8,128)S(1)}, f32[1,6144]{1,0:T(1,128)}, f32[64,256]{1,0:T(8,128)S(1)}, f32[64,256]{1,0:T(8,128)S(1)}, f32[64,256]{1,0:T(8...) custom-call(f32[8,1,6272]{2,1,0:T(1,128)S(1)} %all_to_all.91.refs_0_, s32[1,6144]{1,0:T(1,128)S(1)} %bitcast.13, ...), custom_call_target="tpu_custom_call" | custom-call | tf_op jit(solution)/shard_map/pallas_call | solution.py:34
  177.8 7.7 %all_to_all.92.in_ref = f32[8,24,128]{2,1,0:T(8,128)S(1)} all-to-all(f32[8,24,128]{2,1,0:T(8,128)S(1)} %get-tuple-element.61), channel_id=1, replica_groups=mesh['zh'=8,'zl'=2,'y'=4,'x'=4,'core'=2] {'zl','y'}, dimensions={0} | all-to-all | bytes 196608 | tf_op jit(solution)/shard_map/all_to_all | solution.py:284
  185.5 15.0 %all_to_all.93.in_ref = f32[8,24,128]{2,1,0:T(8,128)S(1)} all-to-all(f32[8,24,128]{2,1,0:T(8,128)S(1)} %shard_map.81), channel_id=1, replica_groups=mesh['zh'=8,'zl'=2,'y'=4,'x'=4,'core'=2] {'zh'}, dimensions={0} | all-to-all | bytes 196608 | tf_op jit(solution)/shard_map/all_to_all | solution.py:284
  200.5 7.7 %all_to_all.94.refs_0_ = f32[8,24,128]{2,1,0:T(8,128)S(1)} all-to-all(f32[8,24,128]{2,1,0:T(8,128)S(1)} %shard_map.82), channel_id=1, replica_groups=mesh['zh'=8,'zl'=2,'y'=4,'x'=4,'core'=2] {'zl','y'}, dimensions={0} | all-to-all | bytes 196608 | tf_op jit(solution)/shard_map/all_to_all | solution.py:284
  208.3 11.7 %all_to_all.95.line_ref = f32[8,1,128]{2,1,0:T(1,128)S(1)} all-to-all(f32[8,1,128]{2,1,0:T(1,128)S(1)} %get-tuple-element.63), channel_id=1, replica_groups=mesh['zh'=8,'zl'=2,'y'=4,'x'=4,'core'=2] {'x','core'}, dimensions={0} | all-to-all | bytes 8192 | tf_op jit(solution)/shard_map/all_to_all | solution.py:284
  (17 shorter events, 3.5 us)
Async XLA Ops:
  0.6 14.6 %copy-start.2 = (f32[6144]{0:T(1024)S(1)}, f32[6144]{0:T(1024)}, u32[]{:S(2)}) copy-start(f32[6144]{0:T(1024)} %param.7) | copy-start | bytes 73732
  0.6 14.6 %copy-start.1 = (s32[6144]{0:T(1024)S(1)}, s32[6144]{0:T(1024)}, u32[]{:S(2)}) copy-start(s32[6144]{0:T(1024)} %param.6) | copy-start | bytes 73732
  1.6 1.9 copy-start

commit v3 on v2

--- a/solution.py
+++ b/solution.py
@@ -17,6 +17,8 @@
 GATHER = 128
 PIECES = 8
 SHARE = TASKS // PIECES
+PAIRS = SHARE // 2
+PIECE = (2 * PAIRS + 1, 2, 128)
 CHUNK = 512
 LINE = ROWS + 128
 
@@ -88,12 +90,13 @@
 def write_pieces(acc_ref, squares, piece_ref):
     total = acc_ref[0:64, :] + acc_ref[64:128, :] + acc_ref[128:192, :]
     back = total[:, :FEATS] - DISCOUNT * total[:, FEATS:]
-    line = jnp.broadcast_to(to_row(jnp.sum(squares, axis=1, keepdims=True)), (8, 128))
+    line = jnp.broadcast_to(to_row(jnp.sum(squares, axis=1, keepdims=True)), (2, 128))
     for piece in range(PIECES):
-        rows = slice(SHARE * piece, SHARE * piece + SHARE)
-        piece_ref[piece, 0:SHARE, :] = back[rows, :128]
-        piece_ref[piece, SHARE : 2 * SHARE, :] = back[rows, 128:]
-        piece_ref[piece, 2 * SHARE :, :] = line
+        for pair in range(PAIRS):
+            row = SHARE * piece + 2 * pair
+            piece_ref[piece, pair] = back[row : row + 2, :128]
+            piece_ref[piece, PAIRS + pair] = back[row : row + 2, 128:]
+        piece_ref[piece, 2 * PAIRS] = line
 
 
 def gather_kernel(first_ref, second_ref, table_ref, ab_ref, wide, left, right):
@@ -148,7 +151,7 @@
     pieces = call(
         first_back_kernel,
         [tasks, rewards, ab],
-        [shaped(PIECES, 24, 128)],
+        [shaped(PIECES, *PIECE)],
         scratch=[pltpu.VMEM((3 * TASKS, 2 * FEATS), F32)],
     )[0]
     return ab, pieces
@@ -163,10 +166,10 @@
 
 
 def raw_right_of(pieces_ref, right_ref):
-    low = jnp.concatenate([pieces_ref[piece, 0:SHARE, :] for piece in range(PIECES)], axis=0)
-    high = jnp.concatenate([pieces_ref[piece, SHARE : 2 * SHARE, :] for piece in range(PIECES)], axis=0)
+    low = jnp.concatenate([pieces_ref[piece, pair] for piece in range(PIECES) for pair in range(PAIRS)], axis=0)
+    high = jnp.concatenate([pieces_ref[piece, PAIRS + pair] for piece in range(PIECES) for pair in range(PAIRS)], axis=0)
     back = jnp.concatenate([low, high], axis=1)
-    left_scale = jnp.sqrt(to_column(pieces_ref[0, 2 * SHARE : 2 * SHARE + 1, :]))
+    left_scale = jnp.sqrt(to_column(pieces_ref[0, 2 * PAIRS, 0:1, :]))
     raw_right = back / left_scale
     if right_ref is not None:
         raw_right = raw_right - left_scale * right_ref[...]
@@ -285,7 +288,7 @@
 
 
 def summed(array, copies):
-    return call(functools.partial(sum_kernel, copies), [array], [shaped(copies, 24, 128)], limit=8)[0]
+    return call(functools.partial(sum_kernel, copies), [array], [shaped(copies, *PIECE)], limit=8)[0]
 
 
 def rows_sum(pieces, sizes):
@@ -315,7 +318,7 @@
         pieces, left, right, *state = call(
             functools.partial(back_kernel, iteration == 0),
             [line, tasks, left, ab, raw, scale] + state,
-            [shaped(PIECES, 24, 128), shaped(1, ROWS), shaped(TASKS, FEATS)]
+            [shaped(PIECES, *PIECE), shaped(1, ROWS), shaped(TASKS, FEATS)]
             + [shaped(TASKS, FEATS)] * 2
             + [shaped(TASKS, 128)] * 2,
             scratch=[pltpu.VMEM((3 * TASKS, 2 * FEATS), F32)],

time: 222 us -> 220 us (level)
  no operation moved by 1% of the time
where the time goes in v3:
time: 220 us; the launch traced here: 219 us
  blocking collectives  187 us (85%)
  Pallas kernels  28.1 us (13%)
    all_to_all x16, blocking collectives, exchange(): return lax.all_to_all(array, axes, 0, 0)  187 us
    pallas_call x18, Pallas kernels, call(): pl.pallas_call(kernel, out_shape=tuple(outs), in_specs=specs or [VMEM] *...  28.1 us

profile of v3, /device:TPU:1, one launch (start us, length us, event | category | flops | bytes accessed | tf_op | source)
XLA Modules:
  0.0 218.9 jit_solution(18084041280993962890)
XLA Ops:
  1.6 1.9 copy-done
  3.5 11.8 %shard_map.67.ab_ref.refs_1_.refs_3_.refs_2_ = bf16[6144,512]{1,0:T(8,128)(2,1)S(1)} custom-call(s32[6144]{0:T(1024)S(1)} %bitcast.17, s32[6144]{0:T(1024)S(1)} %bitcast.16, bf16[6144,256]{1,0:T(8,128)(2,1)S(1)} %copy-done), custom_call_target="tpu_custom_call" | custom-call | tf_op jit(solution)/shard_map/pallas_call | solution.py:36
  16.7 11.4 %all_to_all.80.in_ref = f32[8,9,2,128]{3,2,1,0:T(2,128)S(1)} all-to-all(f32[8,9,2,128]{3,2,1,0:T(2,128)S(1)} %shard_map.68), channel_id=1, replica_groups=mesh['zh'=8,'zl'=2,'y'=4,'x'=4,'core'=2] {'zl','y'}, dimensions={0} | all-to-all | bytes 147456 | tf_op jit(solution)/shard_map/all_to_all | solution.py:287
  28.1 25.9 %all_to_all.81.in_ref = f32[8,9,2,128]{3,2,1,0:T(2,128)S(1)} all-to-all(f32[8,9,2,128]{3,2,1,0:T(2,128)S(1)} %shard_map.69), channel_id=1, replica_groups=mesh['zh'=8,'zl'=2,'y'=4,'x'=4,'core'=2] {'zh'}, dimensions={0} | all-to-all | bytes 147456 | tf_op jit(solution)/shard_map/all_to_all | solution.py:287
  54.1 7.6 %all_to_all.82.refs_0_ = f32[8,9,2,128]{3,2,1,0:T(2,128)S(1)} all-to-all(f32[8,9,2,128]{3,2,1,0:T(2,128)S(1)} %shard_map.70), channel_id=1, replica_groups=mesh['zh'=8,'zl'=2,'y'=4,'x'=4,'core'=2] {'zl','y'}, dimensions={0} | all-to-all | bytes 147456 | tf_op jit(solution)/shard_map/all_to_all | solution.py:287
  61.7 2.3 %shard_map.71 = (f32[8,1,6272]{2,1,0:T(1,128)S(1)}, f32[64,256]{1,0:T(8,128)S(1)}, f32[64,128]{1,0:T(8,128)S(1)}) custom-call(f32[8,9,2,128]{3,2,1,0:T(2,128)S(1)} %all_to_all.82.refs_0_, bf16[6144,512]{1,0:T(8,128)(2,1)S(1)} %shard_map.67.ab_ref.refs_1_.refs_3_.refs_2_, s32[1,6144]{1,0:T(1,128)S(1)} %bitcast.8), custom_call_target="tpu_custom_call" | custom-call | tf_op jit(solution)/shard_map/pallas_call | solution.py:36
  63.9 15.4 %all_to_all.83.refs_0_ = f32[8,1,6272]{2,1,0:T(1,128)S(1)} all-to-all(f32[8,1,6272]{2,1,0:T(1,128)S(1)} %get-tuple-element.38), channel_id=1, replica_groups=mesh['zh'=8,'zl'=2,'y'=4,'x'=4,'core'=2] {'x','core'}, dimensions={0} | all-to-all | bytes 401408 | tf_op jit(solution)/shard_map/all_to_all | solution.py:287
  79.3 2.2 shard_map.72
  81.5 7.6 %all_to_all.84.in_ref = f32[8,9,2,128]{3,2,1,0:T(2,128)S(1)} all-to-all(f32[8,9,2,128]{3,2,1,0:T(2,128)S(1)} %get-tuple-element.41), channel_id=1, replica_groups=mesh['zh'=8,'zl'=2,'y'=4,'x'=4,'core'=2] {'zl','y'}, dimensions={0} | all-to-all | bytes 147456 | tf_op jit(solution)/shard_map/all_to_all | solution.py:287
  89.1 14.7 %all_to_all.85.in_ref = f32[8,9,2,128]{3,2,1,0:T(2,128)S(1)} all-to-all(f32[8,9,2,128]{3,2,1,0:T(2,128)S(1)} %shard_map.73), channel_id=1, replica_groups=mesh['zh'=8,'zl'=2,'y'=4,'x'=4,'core'=2] {'zh'}, dimensions={0} | all-to-all | bytes 147456 | tf_op jit(solution)/shard_map/all_to_all | solution.py:287
  103.8 7.6 %all_to_all.86.refs_0_ = f32[8,9,2,128]{3,2,1,0:T(2,128)S(1)} all-to-all(f32[8,9,2,128]{3,2,1,0:T(2,128)S(1)} %shard_map.74), channel_id=1, replica_groups=mesh['zh'=8,'zl'=2,'y'=4,'x'=4,'core'=2] {'zl','y'}, dimensions={0} | all-to-all | bytes 147456 | tf_op jit(solution)/shard_map/all_to_all | solution.py:287
  111.4 2.2 %shard_map.75 = (f32[8,1,6272]{2,1,0:T(1,128)S(1)}, f32[64,256]{1,0:T(8,128)S(1)}, f32[64,128]{1,0:T(8,128)S(1)}) custom-call(f32[8,9,2,128]{3,2,1,0:T(2,128)S(1)} %all_to_all.86.refs_0_, f32[64,256]{1,0:T(8,128)S(1)} %get-tuple-element.42.refs_1_, bf16[6144,512]{1,0:T(8,128)(2,1)S(1)} %shard_map.67.ab_ref.refs_1_.refs_3_.refs_2_, s32[1,6144]{1,0:T(1,128)S(1)} %bitcast.10), custom_call_target="tpu_custom_call" | custom-call | tf_op jit(solution)/shard_map/pallas_call | solution.py:36
  113.7 12.9 %all_to_all.87.refs_0_ = f32[8,1,6272]{2,1,0:T(1,128)S(1)} all-to-all(f32[8,1,6272]{2,1,0:T(1,128)S(1)} %get-tuple-element.43), channel_id=1, replica_groups=mesh['zh'=8,'zl'=2,'y'=4,'x'=4,'core'=2] {'x','core'}, dimensions={0} | all-to-all | bytes 401408 | tf_op jit(solution)/shard_map/all_to_all | solution.py:287
  126.5 2.2 shard_map.76
  128.7 7.6 %all_to_all.88.in_ref = f32[8,9,2,128]{3,2,1,0:T(2,128)S(1)} all-to-all(f32[8,9,2,128]{3,2,1,0:T(2,128)S(1)} %get-tuple-element.51), channel_id=1, replica_groups=mesh['zh'=8,'zl'=2,'y'=4,'x'=4,'core'=2] {'zl','y'}, dimensions={0} | all-to-all | bytes 147456 | tf_op jit(solution)/shard_map/all_to_all | solution.py:287
  136.4 14.7 %all_to_all.89.in_ref = f32[8,9,2,128]{3,2,1,0:T(2,128)S(1)} all-to-all(f32[8,9,2,128]{3,2,1,0:T(2,128)S(1)} %shard_map.77), channel_id=1, replica_groups=mesh['zh'=8,'zl'=2,'y'=4,'x'=4,'core'=2] {'zh'}, dimensions={0} | all-to-all | bytes 147456 | tf_op jit(solution)/shard_map/all_to_all | solution.py:287
  151.1 7.6 %all_to_all.90.refs_0_ = f32[8,9,2,128]{3,2,1,0:T(2,128)S(1)} all-to-all(f32[8,9,2,128]{3,2,1,0:T(2,128)S(1)} %shard_map.78), channel_id=1, replica_groups=mesh['zh'=8,'zl'=2,'y'=4,'x'=4,'core'=2] {'zl','y'}, dimensions={0} | all-to-all | bytes 147456 | tf_op jit(solution)/shard_map/all_to_all | solution.py:287
  158.7 2.2 %shard_map.79 = (f32[8,1,6272]{2,1,0:T(1,128)S(1)}, f32[64,256]{1,0:T(8,128)S(1)}, f32[64,128]{1,0:T(8,128)S(1)}) custom-call(f32[8,9,2,128]{3,2,1,0:T(2,128)S(1)} %all_to_all.90.refs_0_, f32[64,256]{1,0:T(8,128)S(1)} %get-tuple-element.52.refs_1_, bf16[6144,512]{1,0:T(8,128)(2,1)S(1)} %shard_map.67.ab_ref.refs_1_.refs_3_.refs_2_, s32[1,6144]{1,0:T(1,128)S(1)} %bitcast.12), custom_call_target="tpu_custom_call" | custom-call | tf_op jit(solution)/shard_map/pallas_call | solution.py:36
  160.9 12.9 %all_to_all.91.refs_0_ = f32[8,1,6272]{2,1,0:T(1,128)S(1)} all-to-all(f32[8,1,6272]{2,1,0:T(1,128)S(1)} %get-tuple-element.53), channel_id=1, replica_groups=mesh['zh'=8,'zl'=2,'y'=4,'x'=4,'core'=2] {'x','core'}, dimensions={0} | all-to-all | bytes 401408 | tf_op jit(solution)/shard_map/all_to_all | solution.py:287
  173.8 2.6 %shard_map.80 = (f32[8,9,2,128]{3,2,1,0:T(2,128)S(1)}, f32[1,6144]{1,0:T(1,128)}, f32[64,256]{1,0:T(8,128)S(1)}, f32[64,256]{1,0:T(8,128)S(1)}, f32[64,256]{1,0:...) custom-call(f32[8,1,6272]{2,1,0:T(1,128)S(1)} %all_to_all.91.refs_0_, s32[1,6144]{1,0:T(1,128)S(1)} %bitcast.13, ...), custom_call_target="tpu_custom_call" | custom-call | tf_op jit(solution)/shard_map/pallas_call | solution.py:36
  176.4 7.6 %all_to_all.92.in_ref = f32[8,9,2,128]{3,2,1,0:T(2,128)S(1)} all-to-all(f32[8,9,2,128]{3,2,1,0:T(2,128)S(1)} %get-tuple-element.61), channel_id=1, replica_groups=mesh['zh'=8,'zl'=2,'y'=4,'x'=4,'core'=2] {'zl','y'}, dimensions={0} | all-to-all | bytes 147456 | tf_op jit(solution)/shard_map/all_to_all | solution.py:287
  184.0 14.7 %all_to_all.93.in_ref = f32[8,9,2,128]{3,2,1,0:T(2,128)S(1)} all-to-all(f32[8,9,2,128]{3,2,1,0:T(2,128)S(1)} %shard_map.81), channel_id=1, replica_groups=mesh['zh'=8,'zl'=2,'y'=4,'x'=4,'core'=2] {'zh'}, dimensions={0} | all-to-all | bytes 147456 | tf_op jit(solution)/shard_map/all_to_all | solution.py:287
  198.8 7.6 %all_to_all.94.refs_0_ = f32[8,9,2,128]{3,2,1,0:T(2,128)S(1)} all-to-all(f32[8,9,2,128]{3,2,1,0:T(2,128)S(1)} %shard_map.82), channel_id=1, replica_groups=mesh['zh'=8,'zl'=2,'y'=4,'x'=4,'core'=2] {'zl','y'}, dimensions={0} | all-to-all | bytes 147456 | tf_op jit(solution)/shard_map/all_to_all | solution.py:287
  206.6 11.5 %all_to_all.95.line_ref = f32[8,1,128]{2,1,0:T(1,128)S(1)} all-to-all(f32[8,1,128]{2,1,0:T(1,128)S(1)} %get-tuple-element.63), channel_id=1, replica_groups=mesh['zh'=8,'zl'=2,'y'=4,'x'=4,'core'=2] {'x','core'}, dimensions={0} | all-to-all | bytes 8192 | tf_op jit(solution)/shard_map/all_to_all | solution.py:287
  (17 shorter events, 3.6 us)
Async XLA Ops:
  0.6 14.6 %copy-start.2 = (f32[6144]{0:T(1024)S(1)}, f32[6144]{0:T(1024)}, u32[]{:S(2)}) copy-start(f32[6144]{0:T(1024)} %param.7) | copy-start | bytes 73732
  0.6 14.6 %copy-start.1 = (s32[6144]{0:T(1024)S(1)}, s32[6144]{0:T(1024)}, u32[]{:S(2)}) copy-start(s32[6144]{0:T(1024)} %param.6) | copy-start | bytes 73732
  1.6 1.9 copy-start

commit v4 on v3

--- a/solution.py
+++ b/solution.py
@@ -25,7 +25,7 @@
 F32 = jnp.float32
 BF16 = jnp.bfloat16
 VMEM = pl.BlockSpec(memory_space=pltpu.VMEM)
-SMEM = pl.BlockSpec(memory_space=pltpu.SMEM)
+ANY = pl.BlockSpec(memory_space=pl.ANY)
 
 
 def shaped(*shape, dtype=F32):
@@ -99,7 +99,14 @@
         piece_ref[piece, 2 * PAIRS] = line
 
 
-def gather_kernel(first_ref, second_ref, table_ref, ab_ref, wide, left, right):
+def gather_kernel(first_any, second_any, table_ref, ab_ref, wide, left, right, first_ref, second_ref, sems):
+    loads = [
+        pltpu.make_async_copy(first_any, first_ref, sems.at[0]),
+        pltpu.make_async_copy(second_any, second_ref, sems.at[1]),
+    ]
+    for load in loads:
+        load.start()
+
     def widen(step, carry):
         base = pl.multiple_of(step * 16, 16)
         rows = table_ref[pl.ds(base, 16), :].astype(F32)
@@ -108,23 +115,41 @@
         return carry
 
     lax.fori_loop(0, ROWS // 16, widen, 0, unroll=4)
-
-    def gather(step, carry):
-        base = pl.multiple_of(step * GATHER, GATHER)
-        for row in range(GATHER):
-            current = pl.multiple_of(first_ref[base + row], 2)
-            following = pl.multiple_of(second_ref[base + row], 2)
-            left[2 * row : 2 * row + 2, :] = wide[pl.ds(current, 2), :]
-            right[2 * row : 2 * row + 2, :] = wide[pl.ds(following, 2), :]
-        for half in range(2):
-            lanes = 128 * half
-            ab_ref[pl.ds(base, GATHER), lanes : lanes + 128] = left[pl.ds(half, GATHER, 2), :].astype(BF16)
-            ab_ref[pl.ds(base, GATHER), FEATS + lanes : FEATS + lanes + 128] = right[
-                pl.ds(half, GATHER, 2), :
-            ].astype(BF16)
+    for load in loads:
+        load.wait()
+
+    def fetch(chunk, buffer, first):
+        base = pl.multiple_of(chunk * GATHER, GATHER)
+        for row in range(first, first + 16):
+            for index_ref, lines in ((first_ref, left), (second_ref, right)):
+                at = pl.multiple_of(index_ref[base + row], 2)
+                lines[buffer * 2 * GATHER + 2 * row : buffer * 2 * GATHER + 2 * row + 2, :] = wide[pl.ds(at, 2), :]
+
+    def narrow(chunk, buffer, first):
+        base = pl.multiple_of(chunk * GATHER + first, 16)
+        for side, lines in enumerate((left, right)):
+            for half in range(2):
+                lanes = FEATS * side + 128 * half
+                ab_ref[pl.ds(base, 16), lanes : lanes + 128] = lines[pl.ds(buffer * 2 * GATHER + 2 * first + half, 16, 2), :].astype(BF16)
+
+    def both(chunk, buffer):
+        for first in range(0, GATHER, 16):
+            fetch(chunk, buffer, first)
+            narrow(chunk - 1, 1 - buffer, first)
+
+    for first in range(0, GATHER, 16):
+        fetch(0, 0, first)
+
+    def step(index, carry):
+        both(2 * index + 1, 1)
+        both(2 * index + 2, 0)
         return carry
 
-    lax.fori_loop(0, ROWS // GATHER, gather, 0)
+    chunks = ROWS // GATHER
+    lax.fori_loop(0, chunks // 2 - 1, step, 0)
+    both(chunks - 1, 1)
+    for first in range(0, GATHER, 16):
+        narrow(chunks - 1, 1, first)
 
 
 def first_back_kernel(task_ref, rewards_ref, ab_ref, piece_ref, acc):
@@ -143,10 +168,13 @@
         [shaped(ROWS, 2 * FEATS, dtype=BF16)],
         scratch=[
             pltpu.VMEM((2 * ROWS, 128), F32),
-            pltpu.VMEM((2 * GATHER, 128), F32),
-            pltpu.VMEM((2 * GATHER, 128), F32),
+            pltpu.VMEM((4 * GATHER, 128), F32),
+            pltpu.VMEM((4 * GATHER, 128), F32),
+            pltpu.SMEM((ROWS,), jnp.int32),
+            pltpu.SMEM((ROWS,), jnp.int32),
+            pltpu.SemaphoreType.DMA((2,)),
         ],
-        specs=[SMEM, SMEM, VMEM],
+        specs=[ANY, ANY, VMEM],
     )[0]
     pieces = call(
         first_back_kernel,
@@ -236,13 +264,15 @@
     return (solution[...], direction[...], phi_bar[:, 0:1], rho_bar[:, 0:1])
 
 
-def back_kernel(first, *refs):
+def back_kernel(first, last, *refs):
     refs = list(refs)
     line_ref, task_ref, left_ref, ab_ref, raw_ref, scale_ref = refs[:6]
     refs = refs[6:]
     old_state = None if first else read_state(refs[:4])
     refs = refs if first else refs[4:]
-    piece_ref, new_left_ref, right_ref, solution_ref, direction_ref, phi_ref, rho_ref, acc = refs
+    piece_ref, right_ref, solution_ref, direction_ref, phi_ref, rho_ref = refs[:6]
+    new_left_ref = None if last else refs[6]
+    acc = refs[-1]
     left_scale = scale_ref[:, 0:1]
     right_scale = right_scale_of(line_ref)
     right_vector = raw_ref[...] / right_scale
@@ -258,7 +288,8 @@
         mask = task_mask(task_ref, start)
         raw = product * jnp.sum(jnp.where(mask, by_product, 0.0), axis=0, keepdims=True)
         raw = raw - left_ref[:, pl.ds(start, CHUNK)] * jnp.sum(jnp.where(mask, by_left, 0.0), axis=0, keepdims=True)
-        new_left_ref[:, pl.ds(start, CHUNK)] = raw
+        if not last:
+            new_left_ref[:, pl.ds(start, CHUNK)] = raw
         squares = add_back(index, mask, raw, ab_ref, acc, squares)
     write_pieces(acc, squares, piece_ref)
 
@@ -315,16 +346,19 @@
     state = []
     for iteration in range(ITERS):
         line = exchange(line, feat)
-        pieces, left, right, *state = call(
-            functools.partial(back_kernel, iteration == 0),
+        last = iteration == ITERS - 1
+        pieces, right, *state = call(
+            functools.partial(back_kernel, iteration == 0, last),
             [line, tasks, left, ab, raw, scale] + state,
-            [shaped(PIECES, *PIECE), shaped(1, ROWS), shaped(TASKS, FEATS)]
+            [shaped(PIECES, *PIECE), shaped(TASKS, FEATS)]
             + [shaped(TASKS, FEATS)] * 2
-            + [shaped(TASKS, 128)] * 2,
+            + [shaped(TASKS, 128)] * 2
+            + ([] if last else [shaped(1, ROWS)]),
             scratch=[pltpu.VMEM((3 * TASKS, 2 * FEATS), F32)],
         )
+        if not last:
+            left = state.pop()
         pieces = rows_sum(pieces, sizes)
-        last = iteration == ITERS - 1
         line, raw, scale = call(
             functools.partial(forward_kernel, False, last),
             [pieces, right] + ([] if last else [ab, tasks]),

time: 220 us -> 218 us (level)
  no operation moved by 1% of the time
where the time goes in v4:
time: 218 us; the launch traced here: 217 us
  blocking collectives  187 us (86%)
  Pallas kernels  26.2 us (12%)
    all_to_all x16, blocking collectives, exchange(): return lax.all_to_all(array, axes, 0, 0)  187 us
    pallas_call x18, Pallas kernels, call(): pl.pallas_call(kernel, out_shape=tuple(outs), in_specs=specs or [VMEM] *...  26.2 us

profile of v4, /device:TPU:1, one launch (start us, length us, event | category | flops | bytes accessed | tf_op | source)
XLA Modules:
  0.0 217.0 jit_solution(9787217551775981224)
XLA Ops:
  1.6 1.9 copy-done
  3.5 10.3 %shard_map.67.ab_ref.refs_1_.refs_3_.refs_2_ = bf16[6144,512]{1,0:T(8,128)(2,1)S(1)} custom-call(s32[6144]{0:T(1024)S(1)} %bitcast.17, s32[6144]{0:T(1024)S(1)} %bitcast.16, bf16[6144,256]{1,0:T(8,128)(2,1)S(1)} %copy-done), custom_call_target="tpu_custom_call" | custom-call | tf_op jit(solution)/shard_map/pallas_call | solution.py:36
  15.2 11.4 %all_to_all.80.in_ref = f32[8,9,2,128]{3,2,1,0:T(2,128)S(1)} all-to-all(f32[8,9,2,128]{3,2,1,0:T(2,128)S(1)} %shard_map.68), channel_id=1, replica_groups=mesh['zh'=8,'zl'=2,'y'=4,'x'=4,'core'=2] {'zl','y'}, dimensions={0} | all-to-all | bytes 147456 | tf_op jit(solution)/shard_map/all_to_all | solution.py:318
  26.7 25.9 %all_to_all.81.in_ref = f32[8,9,2,128]{3,2,1,0:T(2,128)S(1)} all-to-all(f32[8,9,2,128]{3,2,1,0:T(2,128)S(1)} %shard_map.69), channel_id=1, replica_groups=mesh['zh'=8,'zl'=2,'y'=4,'x'=4,'core'=2] {'zh'}, dimensions={0} | all-to-all | bytes 147456 | tf_op jit(solution)/shard_map/all_to_all | solution.py:318
  52.6 7.6 %all_to_all.82.refs_0_ = f32[8,9,2,128]{3,2,1,0:T(2,128)S(1)} all-to-all(f32[8,9,2,128]{3,2,1,0:T(2,128)S(1)} %shard_map.70), channel_id=1, replica_groups=mesh['zh'=8,'zl'=2,'y'=4,'x'=4,'core'=2] {'zl','y'}, dimensions={0} | all-to-all | bytes 147456 | tf_op jit(solution)/shard_map/all_to_all | solution.py:318
  60.2 2.3 %shard_map.71 = (f32[8,1,6272]{2,1,0:T(1,128)S(1)}, f32[64,256]{1,0:T(8,128)S(1)}, f32[64,128]{1,0:T(8,128)S(1)}) custom-call(f32[8,9,2,128]{3,2,1,0:T(2,128)S(1)} %all_to_all.82.refs_0_, bf16[6144,512]{1,0:T(8,128)(2,1)S(1)} %shard_map.67.ab_ref.refs_1_.refs_3_.refs_2_, s32[1,6144]{1,0:T(1,128)S(1)} %bitcast.8), custom_call_target="tpu_custom_call" | custom-call | tf_op jit(solution)/shard_map/pallas_call | solution.py:36
  62.5 15.3 %all_to_all.83.refs_0_ = f32[8,1,6272]{2,1,0:T(1,128)S(1)} all-to-all(f32[8,1,6272]{2,1,0:T(1,128)S(1)} %get-tuple-element.38), channel_id=1, replica_groups=mesh['zh'=8,'zl'=2,'y'=4,'x'=4,'core'=2] {'x','core'}, dimensions={0} | all-to-all | bytes 401408 | tf_op jit(solution)/shard_map/all_to_all | solution.py:318
  77.8 2.2 %shard_map.72 = (f32[8,9,2,128]{3,2,1,0:T(2,128)S(1)}, f32[64,256]{1,0:T(8,128)S(1)}, f32[64,256]{1,0:T(8,128)S(1)}, f32[64,256]{1,0:T(8,128)S(1)}, f32[64,128]{...) custom-call(f32[8,1,6272]{2,1,0:T(1,128)S(1)} %all_to_all.83.refs_0_, s32[1,6144]{1,0:T(1,128)S(1)} %bitcast.9, ...), custom_call_target="tpu_custom_call" | custom-call | tf_op jit(solution)/shard_map/pallas_call | solution.py:36
  80.0 7.6 %all_to_all.84.in_ref = f32[8,9,2,128]{3,2,1,0:T(2,128)S(1)} all-to-all(f32[8,9,2,128]{3,2,1,0:T(2,128)S(1)} %get-tuple-element.41), channel_id=1, replica_groups=mesh['zh'=8,'zl'=2,'y'=4,'x'=4,'core'=2] {'zl','y'}, dimensions={0} | all-to-all | bytes 147456 | tf_op jit(solution)/shard_map/all_to_all | solution.py:318
  87.7 14.7 %all_to_all.85.in_ref = f32[8,9,2,128]{3,2,1,0:T(2,128)S(1)} all-to-all(f32[8,9,2,128]{3,2,1,0:T(2,128)S(1)} %shard_map.73), channel_id=1, replica_groups=mesh['zh'=8,'zl'=2,'y'=4,'x'=4,'core'=2] {'zh'}, dimensions={0} | all-to-all | bytes 147456 | tf_op jit(solution)/shard_map/all_to_all | solution.py:318
  102.4 7.6 %all_to_all.86.refs_0_ = f32[8,9,2,128]{3,2,1,0:T(2,128)S(1)} all-to-all(f32[8,9,2,128]{3,2,1,0:T(2,128)S(1)} %shard_map.74), channel_id=1, replica_groups=mesh['zh'=8,'zl'=2,'y'=4,'x'=4,'core'=2] {'zl','y'}, dimensions={0} | all-to-all | bytes 147456 | tf_op jit(solution)/shard_map/all_to_all | solution.py:318
  110.0 2.2 %shard_map.75 = (f32[8,1,6272]{2,1,0:T(1,128)S(1)}, f32[64,256]{1,0:T(8,128)S(1)}, f32[64,128]{1,0:T(8,128)S(1)}) custom-call(f32[8,9,2,128]{3,2,1,0:T(2,128)S(1)} %all_to_all.86.refs_0_, f32[64,256]{1,0:T(8,128)S(1)} %get-tuple-element.42.refs_1_, bf16[6144,512]{1,0:T(8,128)(2,1)S(1)} %shard_map.67.ab_ref.refs_1_.refs_3_.refs_2_, s32[1,6144]{1,0:T(1,128)S(1)} %bitcast.10), custom_call_target="tpu_custom_call" | custom-call | tf_op jit(solution)/shard_map/pallas_call | solution.py:36
  112.2 12.9 %all_to_all.87.refs_0_ = f32[8,1,6272]{2,1,0:T(1,128)S(1)} all-to-all(f32[8,1,6272]{2,1,0:T(1,128)S(1)} %get-tuple-element.43), channel_id=1, replica_groups=mesh['zh'=8,'zl'=2,'y'=4,'x'=4,'core'=2] {'x','core'}, dimensions={0} | all-to-all | bytes 401408 | tf_op jit(solution)/shard_map/all_to_all | solution.py:318
  125.1 2.2 %shard_map.76 = (f32[8,9,2,128]{3,2,1,0:T(2,128)S(1)}, f32[64,256]{1,0:T(8,128)S(1)}, f32[64,256]{1,0:T(8,128)S(1)}, f32[64,256]{1,0:T(8,128)S(1)}, f32[64,128]{...) custom-call(f32[8,1,6272]{2,1,0:T(1,128)S(1)} %all_to_all.87.refs_0_, s32[1,6144]{1,0:T(1,128)S(1)} %bitcast.11, ...), custom_call_target="tpu_custom_call" | custom-call | tf_op jit(solution)/shard_map/pallas_call | solution.py:36
  127.3 7.6 %all_to_all.88.in_ref = f32[8,9,2,128]{3,2,1,0:T(2,128)S(1)} all-to-all(f32[8,9,2,128]{3,2,1,0:T(2,128)S(1)} %get-tuple-element.51), channel_id=1, replica_groups=mesh['zh'=8,'zl'=2,'y'=4,'x'=4,'core'=2] {'zl','y'}, dimensions={0} | all-to-all | bytes 147456 | tf_op jit(solution)/shard_map/all_to_all | solution.py:318
  134.9 14.7 %all_to_all.89.in_ref = f32[8,9,2,128]{3,2,1,0:T(2,128)S(1)} all-to-all(f32[8,9,2,128]{3,2,1,0:T(2,128)S(1)} %shard_map.77), channel_id=1, replica_groups=mesh['zh'=8,'zl'=2,'y'=4,'x'=4,'core'=2] {'zh'}, dimensions={0} | all-to-all | bytes 147456 | tf_op jit(solution)/shard_map/all_to_all | solution.py:318
  149.7 7.6 %all_to_all.90.refs_0_ = f32[8,9,2,128]{3,2,1,0:T(2,128)S(1)} all-to-all(f32[8,9,2,128]{3,2,1,0:T(2,128)S(1)} %shard_map.78), channel_id=1, replica_groups=mesh['zh'=8,'zl'=2,'y'=4,'x'=4,'core'=2] {'zl','y'}, dimensions={0} | all-to-all | bytes 147456 | tf_op jit(solution)/shard_map/all_to_all | solution.py:318
  157.3 2.2 %shard_map.79 = (f32[8,1,6272]{2,1,0:T(1,128)S(1)}, f32[64,256]{1,0:T(8,128)S(1)}, f32[64,128]{1,0:T(8,128)S(1)}) custom-call(f32[8,9,2,128]{3,2,1,0:T(2,128)S(1)} %all_to_all.90.refs_0_, f32[64,256]{1,0:T(8,128)S(1)} %get-tuple-element.52.refs_1_, bf16[6144,512]{1,0:T(8,128)(2,1)S(1)} %shard_map.67.ab_ref.refs_1_.refs_3_.refs_2_, s32[1,6144]{1,0:T(1,128)S(1)} %bitcast.12), custom_call_target="tpu_custom_call" | custom-call | tf_op jit(solution)/shard_map/pallas_call | solution.py:36
  159.5 12.9 %all_to_all.91.refs_0_ = f32[8,1,6272]{2,1,0:T(1,128)S(1)} all-to-all(f32[8,1,6272]{2,1,0:T(1,128)S(1)} %get-tuple-element.53), channel_id=1, replica_groups=mesh['zh'=8,'zl'=2,'y'=4,'x'=4,'core'=2] {'x','core'}, dimensions={0} | all-to-all | bytes 401408 | tf_op jit(solution)/shard_map/all_to_all | solution.py:318
  172.4 2.2 %shard_map.80 = (f32[8,9,2,128]{3,2,1,0:T(2,128)S(1)}, f32[64,256]{1,0:T(8,128)S(1)}, f32[64,256]{1,0:T(8,128)S(1)}, f32[64,256]{1,0:T(8,128)S(1)}, f32[64,128]{1,0:T(8,128)S(1)}, /*index=5*/f32[64,128]{1,0:T(8,128)S(1)}) custom-call(f32[8,1,6272]{2,1,0:T(1,128)S(1)} %all_to_all.91.refs_0_, s32[1,6144]{1,0:T(1,128)S(1)} %bitcast.13, ...), custom_call_target="tpu_custom_call" | custom-call | tf_op jit(solution)/shard_map/pallas_call | solution.py:36
  174.6 7.6 %all_to_all.92.in_ref = f32[8,9,2,128]{3,2,1,0:T(2,128)S(1)} all-to-all(f32[8,9,2,128]{3,2,1,0:T(2,128)S(1)} %get-tuple-element.61), channel_id=1, replica_groups=mesh['zh'=8,'zl'=2,'y'=4,'x'=4,'core'=2] {'zl','y'}, dimensions={0} | all-to-all | bytes 147456 | tf_op jit(solution)/shard_map/all_to_all | solution.py:318
  182.2 14.7 %all_to_all.93.in_ref = f32[8,9,2,128]{3,2,1,0:T(2,128)S(1)} all-to-all(f32[8,9,2,128]{3,2,1,0:T(2,128)S(1)} %shard_map.81), channel_id=1, replica_groups=mesh['zh'=8,'zl'=2,'y'=4,'x'=4,'core'=2] {'zh'}, dimensions={0} | all-to-all | bytes 147456 | tf_op jit(solution)/shard_map/all_to_all | solution.py:318
  196.9 7.6 %all_to_all.94.refs_0_ = f32[8,9,2,128]{3,2,1,0:T(2,128)S(1)} all-to-all(f32[8,9,2,128]{3,2,1,0:T(2,128)S(1)} %shard_map.82), channel_id=1, replica_groups=mesh['zh'=8,'zl'=2,'y'=4,'x'=4,'core'=2] {'zl','y'}, dimensions={0} | all-to-all | bytes 147456 | tf_op jit(solution)/shard_map/all_to_all | solution.py:318
  204.7 11.5 %all_to_all.95.line_ref = f32[8,1,128]{2,1,0:T(1,128)S(1)} all-to-all(f32[8,1,128]{2,1,0:T(1,128)S(1)} %get-tuple-element.63), channel_id=1, replica_groups=mesh['zh'=8,'zl'=2,'y'=4,'x'=4,'core'=2] {'x','core'}, dimensions={0} | all-to-all | bytes 8192 | tf_op jit(solution)/shard_map/all_to_all | solution.py:318
  (17 shorter events, 3.6 us)
Async XLA Ops:
  0.6 13.2 %copy-start.2 = (f32[6144]{0:T(1024)S(1)}, f32[6144]{0:T(1024)}, u32[]{:S(2)}) copy-start(f32[6144]{0:T(1024)} %param.7) | copy-start | bytes 73732
  0.6 13.2 %copy-start.1 = (s32[6144]{0:T(1024)S(1)}, s32[6144]{0:T(1024)}, u32[]{:S(2)}) copy-start(s32[6144]{0:T(1024)} %param.6) | copy-start | bytes 73732
  1.6 1.9 copy-start

commit v5 on v4

--- a/solution.py
+++ b/solution.py
@@ -99,10 +99,10 @@
         piece_ref[piece, 2 * PAIRS] = line
 
 
-def gather_kernel(first_any, second_any, table_ref, ab_ref, wide, left, right, first_ref, second_ref, sems):
+def gather_kernel(pairs_any, table_ref, ab_ref, wide, left, right, first_ref, second_ref, sems):
     loads = [
-        pltpu.make_async_copy(first_any, first_ref, sems.at[0]),
-        pltpu.make_async_copy(second_any, second_ref, sems.at[1]),
+        pltpu.make_async_copy(pairs_any.at[0], first_ref, sems.at[0]),
+        pltpu.make_async_copy(pairs_any.at[1], second_ref, sems.at[1]),
     ]
     for load in loads:
         load.start()
@@ -120,7 +120,7 @@
 
     def fetch(chunk, buffer, first):
         base = pl.multiple_of(chunk * GATHER, GATHER)
-        for row in range(first, first + 16):
+        for row in range(first, first + 8):
             for index_ref, lines in ((first_ref, left), (second_ref, right)):
                 at = pl.multiple_of(index_ref[base + row], 2)
                 lines[buffer * 2 * GATHER + 2 * row : buffer * 2 * GATHER + 2 * row + 2, :] = wide[pl.ds(at, 2), :]
@@ -133,11 +133,12 @@
                 ab_ref[pl.ds(base, 16), lanes : lanes + 128] = lines[pl.ds(buffer * 2 * GATHER + 2 * first + half, 16, 2), :].astype(BF16)
 
     def both(chunk, buffer):
-        for first in range(0, GATHER, 16):
+        for first in range(0, GATHER, 8):
             fetch(chunk, buffer, first)
-            narrow(chunk - 1, 1 - buffer, first)
-
-    for first in range(0, GATHER, 16):
+            if first % 16 == 0:
+                narrow(chunk - 1, 1 - buffer, first)
+
+    for first in range(0, GATHER, 8):
         fetch(0, 0, first)
 
     def step(index, carry):
@@ -148,8 +149,9 @@
     chunks = ROWS // GATHER
     lax.fori_loop(0, chunks // 2 - 1, step, 0)
     both(chunks - 1, 1)
-    for first in range(0, GATHER, 16):
-        narrow(chunks - 1, 1, first)
+    for first in range(0, GATHER, 8):
+        if first % 16 == 0:
+            narrow(chunks - 1, 1, first)
 
 
 def first_back_kernel(task_ref, rewards_ref, ab_ref, piece_ref, acc):
@@ -164,7 +166,7 @@
 def start(pairs, table, tasks, rewards):
     ab = call(
         gather_kernel,
-        [2 * pairs[:, 0], 2 * pairs[:, 1], table],
+        [2 * pairs.T, table],
         [shaped(ROWS, 2 * FEATS, dtype=BF16)],
         scratch=[
             pltpu.VMEM((2 * ROWS, 128), F32),
@@ -174,7 +176,7 @@
             pltpu.SMEM((ROWS,), jnp.int32),
             pltpu.SemaphoreType.DMA((2,)),
         ],
-        specs=[ANY, ANY, VMEM],
+        specs=[ANY, VMEM],
     )[0]
     pieces = call(
         first_back_kernel,

time: 218 us -> 218 us (level)
  no operation moved by 1% of the time
where the time goes in v5:
time: 218 us; the launch traced here: 217 us
  blocking collectives  187 us (86%)
  Pallas kernels  26.2 us (12%)
    all_to_all x16, blocking collectives, exchange(): return lax.all_to_all(array, axes, 0, 0)  187 us
    pallas_call x18, Pallas kernels, call(): pl.pallas_call(kernel, out_shape=tuple(outs), in_specs=specs or [VMEM] *...  26.2 us

profile of v5, /device:TPU:1, one launch (start us, length us, event | category | flops | bytes accessed | tf_op | source)
XLA Modules:
  0.0 216.9 jit_solution(13624042158265216348)
XLA Ops:
  1.5 1.9 copy-done
  3.4 10.3 %shard_map.67.ab_ref.refs_1_.refs_3_.refs_2_ = bf16[6144,512]{1,0:T(8,128)(2,1)S(1)} custom-call(s32[2,6144]{1,0:T(2,128)S(1)} %multiply_bitcast_fusion.pairs_any, bf16[6144,256]{1,0:T(8,128)(2,1)S(1)} %copy-done), custom_call_target="tpu_custom_call" | custom-call | tf_op jit(solution)/shard_map/pallas_call | solution.py:36
  15.1 11.4 %all_to_all.80.in_ref = f32[8,9,2,128]{3,2,1,0:T(2,128)S(1)} all-to-all(f32[8,9,2,128]{3,2,1,0:T(2,128)S(1)} %shard_map.68), channel_id=1, replica_groups=mesh['zh'=8,'zl'=2,'y'=4,'x'=4,'core'=2] {'zl','y'}, dimensions={0} | all-to-all | bytes 147456 | tf_op jit(solution)/shard_map/all_to_all | solution.py:320
  26.5 25.9 %all_to_all.81.in_ref = f32[8,9,2,128]{3,2,1,0:T(2,128)S(1)} all-to-all(f32[8,9,2,128]{3,2,1,0:T(2,128)S(1)} %shard_map.69), channel_id=1, replica_groups=mesh['zh'=8,'zl'=2,'y'=4,'x'=4,'core'=2] {'zh'}, dimensions={0} | all-to-all | bytes 147456 | tf_op jit(solution)/shard_map/all_to_all | solution.py:320
  52.5 7.6 %all_to_all.82.refs_0_ = f32[8,9,2,128]{3,2,1,0:T(2,128)S(1)} all-to-all(f32[8,9,2,128]{3,2,1,0:T(2,128)S(1)} %shard_map.70), channel_id=1, replica_groups=mesh['zh'=8,'zl'=2,'y'=4,'x'=4,'core'=2] {'zl','y'}, dimensions={0} | all-to-all | bytes 147456 | tf_op jit(solution)/shard_map/all_to_all | solution.py:320
  60.1 2.3 %shard_map.71 = (f32[8,1,6272]{2,1,0:T(1,128)S(1)}, f32[64,256]{1,0:T(8,128)S(1)}, f32[64,128]{1,0:T(8,128)S(1)}) custom-call(f32[8,9,2,128]{3,2,1,0:T(2,128)S(1)} %all_to_all.82.refs_0_, bf16[6144,512]{1,0:T(8,128)(2,1)S(1)} %shard_map.67.ab_ref.refs_1_.refs_3_.refs_2_, s32[1,6144]{1,0:T(1,128)S(1)} %bitcast.8), custom_call_target="tpu_custom_call" | custom-call | tf_op jit(solution)/shard_map/pallas_call | solution.py:36
  62.4 15.4 %all_to_all.83.refs_0_ = f32[8,1,6272]{2,1,0:T(1,128)S(1)} all-to-all(f32[8,1,6272]{2,1,0:T(1,128)S(1)} %get-tuple-element.38), channel_id=1, replica_groups=mesh['zh'=8,'zl'=2,'y'=4,'x'=4,'core'=2] {'x','core'}, dimensions={0} | all-to-all | bytes 401408 | tf_op jit(solution)/shard_map/all_to_all | solution.py:320
  77.7 2.2 %shard_map.72 = (f32[8,9,2,128]{3,2,1,0:T(2,128)S(1)}, f32[64,256]{1,0:T(8,128)S(1)}, f32[64,256]{1,0:T(8,128)S(1)}, f32[64,256]{1,0:T(8,128)S(1)}, f32[64,128]{...) custom-call(f32[8,1,6272]{2,1,0:T(1,128)S(1)} %all_to_all.83.refs_0_, s32[1,6144]{1,0:T(1,128)S(1)} %bitcast.9, ...), custom_call_target="tpu_custom_call" | custom-call | tf_op jit(solution)/shard_map/pallas_call | solution.py:36
  79.9 7.6 %all_to_all.84.in_ref = f32[8,9,2,128]{3,2,1,0:T(2,128)S(1)} all-to-all(f32[8,9,2,128]{3,2,1,0:T(2,128)S(1)} %get-tuple-element.41), channel_id=1, replica_groups=mesh['zh'=8,'zl'=2,'y'=4,'x'=4,'core'=2] {'zl','y'}, dimensions={0} | all-to-all | bytes 147456 | tf_op jit(solution)/shard_map/all_to_all | solution.py:320
  87.5 14.7 %all_to_all.85.in_ref = f32[8,9,2,128]{3,2,1,0:T(2,128)S(1)} all-to-all(f32[8,9,2,128]{3,2,1,0:T(2,128)S(1)} %shard_map.73), channel_id=1, replica_groups=mesh['zh'=8,'zl'=2,'y'=4,'x'=4,'core'=2] {'zh'}, dimensions={0} | all-to-all | bytes 147456 | tf_op jit(solution)/shard_map/all_to_all | solution.py:320
  102.3 7.6 %all_to_all.86.refs_0_ = f32[8,9,2,128]{3,2,1,0:T(2,128)S(1)} all-to-all(f32[8,9,2,128]{3,2,1,0:T(2,128)S(1)} %shard_map.74), channel_id=1, replica_groups=mesh['zh'=8,'zl'=2,'y'=4,'x'=4,'core'=2] {'zl','y'}, dimensions={0} | all-to-all | bytes 147456 | tf_op jit(solution)/shard_map/all_to_all | solution.py:320
  109.9 2.2 %shard_map.75 = (f32[8,1,6272]{2,1,0:T(1,128)S(1)}, f32[64,256]{1,0:T(8,128)S(1)}, f32[64,128]{1,0:T(8,128)S(1)}) custom-call(f32[8,9,2,128]{3,2,1,0:T(2,128)S(1)} %all_to_all.86.refs_0_, f32[64,256]{1,0:T(8,128)S(1)} %get-tuple-element.42.refs_1_, bf16[6144,512]{1,0:T(8,128)(2,1)S(1)} %shard_map.67.ab_ref.refs_1_.refs_3_.refs_2_, s32[1,6144]{1,0:T(1,128)S(1)} %bitcast.10), custom_call_target="tpu_custom_call" | custom-call | tf_op jit(solution)/shard_map/pallas_call | solution.py:36
  112.1 12.9 %all_to_all.87.refs_0_ = f32[8,1,6272]{2,1,0:T(1,128)S(1)} all-to-all(f32[8,1,6272]{2,1,0:T(1,128)S(1)} %get-tuple-element.43), channel_id=1, replica_groups=mesh['zh'=8,'zl'=2,'y'=4,'x'=4,'core'=2] {'x','core'}, dimensions={0} | all-to-all | bytes 401408 | tf_op jit(solution)/shard_map/all_to_all | solution.py:320
  125.0 2.2 %shard_map.76 = (f32[8,9,2,128]{3,2,1,0:T(2,128)S(1)}, f32[64,256]{1,0:T(8,128)S(1)}, f32[64,256]{1,0:T(8,128)S(1)}, f32[64,256]{1,0:T(8,128)S(1)}, f32[64,128]{...) custom-call(f32[8,1,6272]{2,1,0:T(1,128)S(1)} %all_to_all.87.refs_0_, s32[1,6144]{1,0:T(1,128)S(1)} %bitcast.11, ...), custom_call_target="tpu_custom_call" | custom-call | tf_op jit(solution)/shard_map/pallas_call | solution.py:36
  127.2 7.6 %all_to_all.88.in_ref = f32[8,9,2,128]{3,2,1,0:T(2,128)S(1)} all-to-all(f32[8,9,2,128]{3,2,1,0:T(2,128)S(1)} %get-tuple-element.51), channel_id=1, replica_groups=mesh['zh'=8,'zl'=2,'y'=4,'x'=4,'core'=2] {'zl','y'}, dimensions={0} | all-to-all | bytes 147456 | tf_op jit(solution)/shard_map/all_to_all | solution.py:320
  134.8 14.7 %all_to_all.89.in_ref = f32[8,9,2,128]{3,2,1,0:T(2,128)S(1)} all-to-all(f32[8,9,2,128]{3,2,1,0:T(2,128)S(1)} %shard_map.77), channel_id=1, replica_groups=mesh['zh'=8,'zl'=2,'y'=4,'x'=4,'core'=2] {'zh'}, dimensions={0} | all-to-all | bytes 147456 | tf_op jit(solution)/shard_map/all_to_all | solution.py:320
  149.6 7.6 %all_to_all.90.refs_0_ = f32[8,9,2,128]{3,2,1,0:T(2,128)S(1)} all-to-all(f32[8,9,2,128]{3,2,1,0:T(2,128)S(1)} %shard_map.78), channel_id=1, replica_groups=mesh['zh'=8,'zl'=2,'y'=4,'x'=4,'core'=2] {'zl','y'}, dimensions={0} | all-to-all | bytes 147456 | tf_op jit(solution)/shard_map/all_to_all | solution.py:320
  157.2 2.2 %shard_map.79 = (f32[8,1,6272]{2,1,0:T(1,128)S(1)}, f32[64,256]{1,0:T(8,128)S(1)}, f32[64,128]{1,0:T(8,128)S(1)}) custom-call(f32[8,9,2,128]{3,2,1,0:T(2,128)S(1)} %all_to_all.90.refs_0_, f32[64,256]{1,0:T(8,128)S(1)} %get-tuple-element.52.refs_1_, bf16[6144,512]{1,0:T(8,128)(2,1)S(1)} %shard_map.67.ab_ref.refs_1_.refs_3_.refs_2_, s32[1,6144]{1,0:T(1,128)S(1)} %bitcast.12), custom_call_target="tpu_custom_call" | custom-call | tf_op jit(solution)/shard_map/pallas_call | solution.py:36
  159.4 12.9 %all_to_all.91.refs_0_ = f32[8,1,6272]{2,1,0:T(1,128)S(1)} all-to-all(f32[8,1,6272]{2,1,0:T(1,128)S(1)} %get-tuple-element.53), channel_id=1, replica_groups=mesh['zh'=8,'zl'=2,'y'=4,'x'=4,'core'=2] {'x','core'}, dimensions={0} | all-to-all | bytes 401408 | tf_op jit(solution)/shard_map/all_to_all | solution.py:320
  172.2 2.2 %shard_map.80 = (f32[8,9,2,128]{3,2,1,0:T(2,128)S(1)}, f32[64,256]{1,0:T(8,128)S(1)}, f32[64,256]{1,0:T(8,128)S(1)}, f32[64,256]{1,0:T(8,128)S(1)}, f32[64,128]{1,0:T(8,128)S(1)}, /*index=5*/f32[64,128]{1,0:T(8,128)S(1)}) custom-call(f32[8,1,6272]{2,1,0:T(1,128)S(1)} %all_to_all.91.refs_0_, s32[1,6144]{1,0:T(1,128)S(1)} %bitcast.13, ...), custom_call_target="tpu_custom_call" | custom-call | tf_op jit(solution)/shard_map/pallas_call | solution.py:36
  174.4 7.6 %all_to_all.92.in_ref = f32[8,9,2,128]{3,2,1,0:T(2,128)S(1)} all-to-all(f32[8,9,2,128]{3,2,1,0:T(2,128)S(1)} %get-tuple-element.61), channel_id=1, replica_groups=mesh['zh'=8,'zl'=2,'y'=4,'x'=4,'core'=2] {'zl','y'}, dimensions={0} | all-to-all | bytes 147456 | tf_op jit(solution)/shard_map/all_to_all | solution.py:320
  182.1 14.7 %all_to_all.93.in_ref = f32[8,9,2,128]{3,2,1,0:T(2,128)S(1)} all-to-all(f32[8,9,2,128]{3,2,1,0:T(2,128)S(1)} %shard_map.81), channel_id=1, replica_groups=mesh['zh'=8,'zl'=2,'y'=4,'x'=4,'core'=2] {'zh'}, dimensions={0} | all-to-all | bytes 147456 | tf_op jit(solution)/shard_map/all_to_all | solution.py:320
  196.8 7.6 %all_to_all.94.refs_0_ = f32[8,9,2,128]{3,2,1,0:T(2,128)S(1)} all-to-all(f32[8,9,2,128]{3,2,1,0:T(2,128)S(1)} %shard_map.82), channel_id=1, replica_groups=mesh['zh'=8,'zl'=2,'y'=4,'x'=4,'core'=2] {'zl','y'}, dimensions={0} | all-to-all | bytes 147456 | tf_op jit(solution)/shard_map/all_to_all | solution.py:320
  204.6 11.5 %all_to_all.95.line_ref = f32[8,1,128]{2,1,0:T(1,128)S(1)} all-to-all(f32[8,1,128]{2,1,0:T(1,128)S(1)} %get-tuple-element.63), channel_id=1, replica_groups=mesh['zh'=8,'zl'=2,'y'=4,'x'=4,'core'=2] {'x','core'}, dimensions={0} | all-to-all | bytes 8192 | tf_op jit(solution)/shard_map/all_to_all | solution.py:320
  (17 shorter events, 3.5 us)
Async XLA Ops:
  0.6 13.1 %copy-start.2 = (f32[6144]{0:T(1024)S(1)}, f32[6144]{0:T(1024)}, u32[]{:S(2)}) copy-start(f32[6144]{0:T(1024)} %param.7) | copy-start | bytes 73732
  0.6 13.1 %copy-start.1 = (s32[6144]{0:T(1024)S(1)}, s32[6144]{0:T(1024)}, u32[]{:S(2)}) copy-start(s32[6144]{0:T(1024)} %param.6) | copy-start | bytes 73732
  1.5 1.9 copy-start
